TPU v7x, 32 devices: a whole 2x2x4 slice. The times are simulated.
32 devices in a mesh: seq: 8 (over z, core), fsdp: 4 (over y, x).
Axes of the slice: x: 2, y: 2, z: 4, core: 2. Of those that a mesh axis runs over, the one named last changes fastest.
Arguments:
- tokens: bfloat16 [4, 1024, 4096], P('fsdp', 'seq'), may hold values from -40 to 40
- cotangent: bfloat16 [4, 1024, 4096], P('fsdp', 'seq'), may hold values from -6 to 6
- w_query: bfloat16 [4096, 2048], P(None, 'fsdp'), may hold values from -0.09375 to 0.09375
- w_key: bfloat16 [4096, 2048], P(None, 'fsdp'), may hold values from -0.09375 to 0.09375
- w_value: bfloat16 [4096, 2048], P(None, 'fsdp'), may hold values from -0.09375 to 0.09375
- w_output: bfloat16 [2048, 4096], P('fsdp'), may hold values from -0.125 to 0.125
- global_pos: int32 [4, 128], replicated, may hold values from 0 to 1023
- pattern: int32 [4, 16, 2], P(None, 'seq'), may hold values 0 or 1
Outputs:
- grad_tokens: bfloat16 [4, 1024, 4096], P('fsdp', 'seq')
- grad_query: float32 [4096, 2048], P('seq', 'fsdp')
- grad_key: float32 [4096, 2048], P('seq', 'fsdp')
- grad_value: float32 [4096, 2048], P('seq', 'fsdp')
- grad_output: float32 [2048, 4096], P('fsdp', 'seq')
All inputs are finite; a program needn't handle non-finite values. No bound on the sum of `pattern` on one device may be relied on, other than what follows from the above.
Results may differ from a plain program's by a relative error of at most 0.019.
Values may be sent and summed in bfloat16 or wider, within the bound.
No kernel may reach another device: no remote copies, remote signals or barrier semaphores. Data moves between devices by JAX's collectives and lax.ppermute only.
A program may use at most 192 MiB of HBM per device.

v0:
```python
import jax
import jax.numpy as jnp
from jax import lax
from jax.sharding import PartitionSpec as P

HDIM = 128
BLOCK = 64


def with_halo(value, sides, width):
    for axis, dim in sides:
        devices, length = (lax.axis_size(axis), value.shape[dim])
        up = [(i, (i + 1) % devices) for i in range(devices - 1)]
        down = [(j, i) for i, j in up]
        last = lax.slice_in_dim(value, length - width, length, axis=dim)
        leading = lax.slice_in_dim(value, 0, width, axis=dim)
        before = lax.ppermute(last, axis, up)
        after = lax.ppermute(leading, axis, down)
        value = jnp.concatenate([before, value, after], axis=dim)
    return value


def product(form, left, right):
    return jnp.einsum(form, left, right, preferred_element_type=jnp.float32)


def block_mask(pattern, first_block, block_total):
    block_count = pattern.shape[0]
    index = first_block + jnp.arange(block_count, dtype=jnp.int32)
    before = (pattern[:, 0] == 1) & (index > 0)
    after = (pattern[:, 1] == 1) & (index < block_total - 1)
    middle = jnp.ones((block_count, BLOCK), jnp.bool_)
    return jnp.concatenate(
        [
            jnp.broadcast_to(before[:, None], (block_count, BLOCK)),
            middle,
            jnp.broadcast_to(after[:, None], (block_count, BLOCK)),
        ],
        axis=1,
    )


def windows(extended, block_count):
    blocks = extended.reshape(block_count + 2, BLOCK, extended.shape[-1])
    return jnp.concatenate([blocks[:block_count], blocks[1 : block_count + 1], blocks[2:]], axis=1)


def unwindow(grads, block_count):
    lower = grads[:, :BLOCK]
    center = grads[:, BLOCK : 2 * BLOCK]
    upper = grads[:, 2 * BLOCK :]
    summed = jnp.pad(lower, ((0, 2), (0, 0), (0, 0))) + jnp.pad(center, ((1, 1), (0, 0), (0, 0)))
    summed = summed + jnp.pad(upper, ((2, 0), (0, 0), (0, 0)))
    return summed.reshape((block_count + 2) * BLOCK, grads.shape[-1])


def doc_attention(query, extended, global_kv, pattern, grad_ctx, first_block, block_total):
    row_count, head_width = query.shape
    block_count = row_count // BLOCK
    head_count = head_width // HDIM
    scale = HDIM ** (-0.5)
    window_kv = windows(extended, block_count)
    key_win = window_kv[..., :head_width].reshape(block_count, 3 * BLOCK, head_count, HDIM)
    value_win = window_kv[..., head_width:].reshape(block_count, 3 * BLOCK, head_count, HDIM)
    key_glob = global_kv[:, :head_width].reshape(-1, head_count, HDIM)
    value_glob = global_kv[:, head_width:].reshape(-1, head_count, HDIM)
    queries = query.reshape(block_count, BLOCK, head_count, HDIM)
    grad_out = grad_ctx.reshape(block_count, BLOCK, head_count, HDIM)
    mask = block_mask(pattern, first_block, block_total)
    local = product("nqhe,nkhe->nhqk", queries, key_win) * scale
    local = jnp.where(mask[:, None, None, :], local, -jnp.inf)
    remote = product("nqhe,ghe->nhqg", queries, key_glob) * scale
    top = jnp.maximum(local.max(-1), remote.max(-1))[..., None]
    local_exp = jnp.exp(local - top)
    remote_exp = jnp.exp(remote - top)
    denom = local_exp.sum(-1, keepdims=True) + remote_exp.sum(-1, keepdims=True)
    p_local = local_exp / denom
    p_remote = remote_exp / denom
    p_local_b = p_local.astype(jnp.bfloat16)
    p_remote_b = p_remote.astype(jnp.bfloat16)
    context = (
        product("nhqk,nkhe->nqhe", p_local_b, value_win)
        + product("nhqg,ghe->nqhe", p_remote_b, value_glob)
    ).astype(jnp.bfloat16)
    d_local = product("nqhe,nkhe->nhqk", grad_out, value_win)
    d_remote = product("nqhe,ghe->nhqg", grad_out, value_glob)
    delta = (p_local * d_local).sum(-1, keepdims=True) + (p_remote * d_remote).sum(
        -1, keepdims=True
    )
    s_local = (p_local * (d_local - delta) * scale).astype(jnp.bfloat16)
    s_remote = (p_remote * (d_remote - delta) * scale).astype(jnp.bfloat16)
    grad_q = (
        product("nhqk,nkhe->nqhe", s_local, key_win) + product("nhqg,ghe->nqhe", s_remote, key_glob)
    ).astype(jnp.bfloat16)
    dkey_win = product("nhqk,nqhe->nkhe", s_local, queries)
    dvalue_win = product("nhqk,nqhe->nkhe", p_local_b, grad_out)
    dkey_glob = product("nhqg,nqhe->ghe", s_remote, queries)
    dvalue_glob = product("nhqg,nqhe->ghe", p_remote_b, grad_out)
    grad_ext = unwindow(
        jnp.concatenate(
            [
                dkey_win.reshape(block_count, 3 * BLOCK, head_width),
                dvalue_win.reshape(block_count, 3 * BLOCK, head_width),
            ],
            -1,
        ),
        block_count,
    )
    grad_glob = jnp.concatenate(
        [dkey_glob.reshape(-1, head_width), dvalue_glob.reshape(-1, head_width)], -1
    )
    return (
        context.reshape(row_count, head_width),
        grad_q.reshape(row_count, head_width),
        grad_ext,
        grad_glob,
    )


def contract_rows(left, right):
    return lax.dot_general(
        left, right, (((0,), (0,)), ((), ())), preferred_element_type=jnp.float32
    )


def contract_cols(left, right):
    return lax.dot_general(
        left, right, (((1,), (1,)), ((), ())), preferred_element_type=jnp.float32
    )


def on_device(tokens, cotangent, w_query, w_key, w_value, w_output, global_pos, pattern):
    inputs = lax.all_gather(tokens, "fsdp", axis=0, tiled=True)
    doc_count, row_count, model_width = inputs.shape
    head_width = w_query.shape[1]
    flat = inputs.reshape(doc_count * row_count, model_width)
    query = jnp.dot(flat, w_query, preferred_element_type=jnp.float32).astype(jnp.bfloat16)
    keys = jnp.dot(flat, w_key, preferred_element_type=jnp.float32).astype(jnp.bfloat16)
    value_rows = jnp.dot(flat, w_value, preferred_element_type=jnp.float32).astype(jnp.bfloat16)
    keys_vals = jnp.concatenate([keys, value_rows], -1).reshape(
        doc_count, row_count, 2 * head_width
    )
    extended = with_halo(keys_vals, (("seq", 1),), BLOCK)
    seq_start = lax.axis_index("seq") * row_count
    selector = (
        global_pos[:, :, None] - seq_start == jnp.arange(row_count, dtype=jnp.int32)[None, None, :]
    )
    picked = jnp.einsum(
        "bgt,btc->bgc", selector.astype(jnp.bfloat16), keys_vals, preferred_element_type=jnp.float32
    )
    global_kv = lax.psum(picked.astype(jnp.bfloat16), "seq")
    grads_in = lax.all_gather(cotangent, "fsdp", axis=0, tiled=True)
    grads_flat = grads_in.reshape(doc_count * row_count, model_width)
    grad_ctx = contract_cols(grads_flat, w_output).astype(jnp.bfloat16)
    block_count = row_count // BLOCK
    first_block = lax.axis_index("seq") * block_count
    block_total = block_count * lax.axis_size("seq")
    context, grad_q, grad_ext, grad_glob = jax.vmap(
        doc_attention, in_axes=(0, 0, 0, 0, 0, None, None)
    )(
        query.reshape(doc_count, row_count, head_width),
        extended,
        global_kv,
        pattern,
        grad_ctx.reshape(doc_count, row_count, head_width),
        first_block,
        block_total,
    )
    rims = jnp.concatenate([grad_ext[:, :BLOCK], grad_ext[:, row_count + BLOCK :]], 1)
    received = with_halo(rims, (("seq", 1),), BLOCK)
    owned = grad_ext[:, BLOCK : row_count + BLOCK]
    owned = owned + jnp.pad(received[:, :BLOCK], ((0, 0), (0, row_count - BLOCK), (0, 0)))
    owned = owned + jnp.pad(received[:, 3 * BLOCK :], ((0, 0), (row_count - BLOCK, 0), (0, 0)))
    glob_sum = lax.psum(grad_glob, "seq")
    owned = owned + jnp.einsum(
        "bgt,bgc->btc", selector.astype(jnp.float32), glob_sum, precision=lax.Precision.HIGHEST
    )
    flat_q = grad_q.reshape(doc_count * row_count, head_width)
    flat_k = owned[..., :head_width].astype(jnp.bfloat16).reshape(doc_count * row_count, head_width)
    flat_v = owned[..., head_width:].astype(jnp.bfloat16).reshape(doc_count * row_count, head_width)
    flat_ctx = context.reshape(doc_count * row_count, head_width)
    partial_value = (
        contract_cols(flat_q, w_query)
        + contract_cols(flat_k, w_key)
        + contract_cols(flat_v, w_value)
    ).reshape(doc_count, row_count, model_width)
    grad_tokens = lax.psum_scatter(
        partial_value.astype(jnp.bfloat16), "fsdp", scatter_dimension=0, tiled=True
    )
    whole_term = jnp.concatenate(
        [
            contract_rows(flat, flat_q),
            contract_rows(flat, flat_k),
            contract_rows(flat, flat_v),
            contract_rows(grads_flat, flat_ctx),
        ],
        1,
    )
    shares = lax.psum_scatter(
        whole_term.astype(jnp.bfloat16), "seq", scatter_dimension=0, tiled=True
    ).astype(jnp.float32)
    grad_query = shares[:, :head_width]
    grad_key = shares[:, head_width : 2 * head_width]
    grad_value = shares[:, 2 * head_width : 3 * head_width]
    grad_output = shares[:, 3 * head_width :].T
    return (grad_tokens, grad_query, grad_key, grad_value, grad_output)


def solution(mesh):
    in_specs = (
        P("fsdp", "seq", None),
        P("fsdp", "seq", None),
        P(None, "fsdp"),
        P(None, "fsdp"),
        P(None, "fsdp"),
        P("fsdp", None),
        P(),
        P(None, "seq", None),
    )
    out_specs = (
        P("fsdp", "seq", None),
        P("seq", "fsdp"),
        P("seq", "fsdp"),
        P("seq", "fsdp"),
        P("fsdp", "seq"),
    )
    return jax.shard_map(
        on_device, mesh=mesh, in_specs=in_specs, out_specs=out_specs, check_vma=False
    )
```

profile of v0, /device:TPU:0, one launch (start us, length us, event | category | flops | bytes accessed | tf_op | source)
XLA Modules:
  0.0 543.0 jit_solution(3749814106811923121)
XLA Ops:
  10.8 54.5 %all-gather.3.cloned.1.call-done = bf16[4,128,4096]{2,1,0:T(8,128)(2,1)} async-done(((bf16[1,128,4096]{2,1,0:T(8,128)(2,1)}), bf16[4,128,4096]{2,1,0:T(8,128)(2,1)}) %all-gather.3.cloned.1.call-update) | async-done | bytes 4194320 | tf_op jit(solution)/shard_map/all_gather | solution.py:133
  65.3 6.0 %convolution_convert_fusion.5 = bf16[512,512]{0,1:T(8,128)(2,1)S(1)} fusion(bf16[512,4096]{1,0:T(8,128)(2,1)} %bitcast.163, bf16[4096,512]{1,0:T(8,128)(2,1)} %param.12), kind=kOutput, calls=%fused_computation.52 | convolution fusion | flops 2147745792 | bytes 8912896 | tf_op jit(solution)/shard_map/dot_general | solution.py:139
  71.3 2.4 convolution_convert_fusion.6
  75.7 6.0 %convolution_convert_fusion.4 = bf16[512,512]{1,0:T(8,128)(2,1)S(1)} fusion(bf16[512,4096]{1,0:T(8,128)(2,1)} %bitcast.164, bf16[4096,512]{1,0:T(8,128)(2,1)} %param.10), kind=kOutput, calls=%fused_computation.51 | convolution fusion | flops 2147745792 | bytes 8912896 | tf_op jit(solution)/shard_map/dot_general | solution.py:137
  81.9 38.0 %all-gather.5.cloned.1.call-done = bf16[4,128,4096]{2,1,0:T(8,128)(2,1)} async-done(((bf16[1,128,4096]{2,1,0:T(8,128)(2,1)}), bf16[4,128,4096]{2,1,0:T(8,128)(2,1)}) %all-gather.5.cloned.1.call-update) | async-done | bytes 4194320 | tf_op jit(solution)/shard_map/all_gather | solution.py:152
  119.9 5.8 %convolution_convert_fusion.3 = bf16[512,512]{1,0:T(8,128)(2,1)S(1)} fusion(bf16[512,4096]{1,0:T(8,128)(2,1)} %bitcast.179, bf16[512,4096]{1,0:T(8,128)(2,1)} %param.13), kind=kOutput, calls=%fused_computation.50 | convolution fusion | flops 2147745792 | bytes 8912896 | tf_op jit(solution)/shard_map/dot_general | solution.py:127
  127.3 2.6 collective-permute-start
  131.4 51.3 %all-reduce.9.cloned.1.call-done = bf16[4,128,1024]{2,1,0:T(8,128)(2,1)} async-done(((bf16[4,128,1024]{2,1,0:T(8,128)(2,1)}), bf16[4,128,1024]{2,1,0:T(8,128)(2,1)}) %all-reduce.9.cloned.1.call-update) | async-done | bytes 1048592 | tf_op jit(solution)/shard_map/psum | solution.py:151
  182.6 2.5 fusion.77
  195.5 3.0 convolution_bitcast_fusion
  205.2 2.0 reshape.112
  207.2 2.0 reshape.109
  209.2 2.5 fusion.65
  211.7 2.5 copy.195
  214.2 2.0 fusion.31
  220.7 2.5 copy.194
  223.2 3.1 pad_maximum_fusion.3
  235.0 4.4 fusion.1
  239.4 4.3 fusion
  243.7 52.0 %all-reduce.11.cloned.1.call-done = f32[4,128,1024]{2,1,0:T(8,128)} async-done(((f32[4,128,1024]{2,1,0:T(8,128)}), f32[4,128,1024]{2,1,0:T(8,128)}) %all-reduce.11.cloned.1.call-update) | async-done | bytes 2097168 | tf_op jit(solution)/shard_map/psum | solution.py:174
  295.8 4.0 fusion.6
  299.7 2.4 fusion.3
  302.1 2.4 fusion.2
  305.6 7.6 %pad_maximum_fusion = bf16[4096,2048]{0,1:T(8,128)(2,1)} fusion(bf16[4096,512]{0,1:T(8,128)(2,1)S(1)} %copy-done.4, bf16[4096,512]{0,1:T(8,128)(2,1)S(1)} %fusion.3, bf16[4096,512]{0,1:T(8,128)(2,1)S(1)} %fusion.2, bf16[4096,512]{0,1:T(8,128)(2,1)S(1)} %copy-done.5), kind=kLoop, calls=%fused_computation | loop fusion | flops 67108864 | bytes 33554432 | tf_op jit(solution)/shard_map/concatenate | solution.py:190
  313.5 4.7 fusion.38
  318.3 5.7 %fusion.81 = f32[512,4096]{1,0:T(8,128)} fusion(bf16[512,512]{1,0:T(8,128)(2,1)S(1)} %bitcast.187, bf16[4096,512]{1,0:T(8,128)(2,1)S(1)} %copy-done.17), kind=kOutput, calls=%fused_computation.119 | convolution fusion | flops 2147483648 | bytes 13107200 | tf_op jit(solution)/shard_map/dot_general | solution.py:127
  324.0 7.8 %add_convert_fusion = bf16[512,4096]{1,0:T(8,128)(2,1)} fusion(f32[512,4096]{1,0:T(8,128)S(1)} %fusion.38, f32[512,4096]{1,0:T(8,128)} %fusion.81, bf16[512,512]{1,0:T(8,128)(2,1)S(1)} %bitcast.186, bf16[4096,512]{1,0:T(8,128)(2,1)S(1)} %copy-done.18), kind=kOutput, calls=%fused_computation.3 | convolution fusion | flops 2153775104 | bytes 25690112 | tf_op jit(solution)/shard_map/dot_general | solution.py:127
  331.8 149.4 %reduce-scatter.5.cloned.1.call-done = bf16[512,2048]{0,1:T(8,128)(2,1)} async-done(((bf16[4096,2048]{0,1:T(8,128)(2,1)}), bf16[512,2048]{0,1:T(8,128)(2,1)}) %reduce-scatter.5.cloned.1.call-update) | async-done | bytes 2097168 | tf_op jit(solution)/shard_map/reduce_scatter | solution.py:199
  481.2 3.1 fusion.75
  484.3 2.7 copy.204
  487.0 2.5 copy.203
  492.5 43.2 %reduce-scatter.7.cloned.1.call-done = bf16[1,128,4096]{2,1,0:T(8,128)(2,1)} async-done(((bf16[4,128,4096]{2,1,0:T(8,128)(2,1)}), bf16[1,128,4096]{2,1,0:T(8,128)(2,1)}) %reduce-scatter.7.cloned.1.call-update) | async-done | bytes 1048592
  (124 shorter events, 43.1 us)
Async XLA Ops:
  7.2 58.1 %all-gather.3.cloned.1.call-start = ((), (), s32[]{:S(2)}) async-start(), calls=%async_computation.2 | async-start | bytes 5242880 | tf_op jit(solution)/shard_map/all_gather | solution.py:133
  7.9 112.0 %all-gather.5.cloned.1.call-start = ((), (), s32[]{:S(2)}) async-start(), calls=%async_computation.4 | async-start | bytes 5242880 | tf_op jit(solution)/shard_map/all_gather | solution.py:152
  8.6 174.0 %all-reduce.9.cloned.1.call-start = ((), (), s32[]{:S(2)}) async-start(), calls=%async_computation.3 | async-start | bytes 2097152 | tf_op jit(solution)/shard_map/psum | solution.py:151
  65.3 6.0 %copy-start = (bf16[4,128,4096]{2,1,0:T(8,128)(2,1)S(1)}, bf16[4,128,4096]{2,1,0:T(8,128)(2,1)}, u32[]{:S(2)}) copy-start(bf16[4,128,4096]{2,1,0:T(8,128)(2,1)} %all-gather.3.cloned.1.call-done) | copy-start | bytes 12582916
  65.3 6.0 %copy-start.16 = (bf16[4096,512]{1,0:T(8,128)(2,1)S(1)}, bf16[4096,512]{1,0:T(8,128)(2,1)}, u32[]{:S(2)}) copy-start(bf16[4096,512]{1,0:T(8,128)(2,1)} %param.11) | copy-start | bytes 12582916
  81.8 213.9 %all-reduce.11.cloned.1.call-start = ((), (), s32[]{:S(2)}) async-start(), calls=%async_computation.5 | async-start | bytes 4194304 | tf_op jit(solution)/shard_map/psum | solution.py:174
  125.8 69.7 %copy-start.15 = (bf16[4,2,64,4,128]{4,3,2,1,0:T(4,128)(2,1)}, bf16[4,2,64,4,128]{4,3,2,1,0:T(4,128)(2,1)S(1)}, u32[]{:S(2)}) copy-start(bf16[4,2,64,4,128]{4,3,2,1,0:T(4,128)(2,1)S(1)} %reshape_reshape.7) | copy-start | bytes 1572868
  126.1 62.8 %copy-start.11 = (bf16[4,2,64,4,128]{4,3,2,1,0:T(4,128)(2,1)}, bf16[4,2,64,4,128]{4,3,2,1,0:T(4,128)(2,1)S(1)}, u32[]{:S(2)}) copy-start(bf16[4,2,64,4,128]{4,3,2,1,0:T(4,128)(2,1)S(1)} %reshape_reshape.6) | copy-start | bytes 1572868
  127.3 58.7 %collective-permute-start = (bf16[4,64,1024]{2,1,0:T(8,128)(2,1)}, bf16[4,64,1024]{2,1,0:T(8,128)(2,1)}, u32[]{:S(2)}, u32[]{:S(2)}) collective-permute-start(bf16[4,64,1024]{2,1,0:T(8,128)(2,1)} %get-tuple-element.51), channel_id=1, source_target_pairs={{0,4},{4,8},{8,12},{12,16},{16,20},{20,24},{24,28},{1,5},{5,9},{9,... | collective-permute-start | bytes 1572872 | tf_op jit(solution)/shard_map/ppermute | solution.py:17
  129.9 56.1 %collective-permute-start.1 = (bf16[4,64,1024]{2,1,0:T(8,128)(2,1)}, bf16[4,64,1024]{2,1,0:T(8,128)(2,1)}, u32[]{:S(2)}, u32[]{:S(2)}) collective-permute-start(bf16[4,64,1024]{2,1,0:T(8,128)(2,1)} %get-tuple-element.52), channel_id=1, source_target_pairs={{4,0},{8,4},{12,8},{16,12},{20,16},{24,20},{28,24},{5,1},{9,5},{13... | collective-permute-start | bytes 1572872 | tf_op jit(solution)/shard_map/ppermute | solution.py:18
  199.9 1.8 copy-start.9
  214.2 3.2 copy-start.8
  214.2 3.2 copy-start.10
  214.2 3.6 copy-start.13
  216.2 2.9 copy-start.19
  216.2 2.9 copy-start.23
  226.3 254.9 %reduce-scatter.5.cloned.1.call-start = ((), (), s32[]{:S(2)}) async-start(), calls=%async_computation.6 | async-start | bytes 18874368 | tf_op jit(solution)/shard_map/reduce_scatter | solution.py:199
  226.5 1.9 copy-start.21
  229.7 5.3 copy-start.22
  230.7 8.7 %copy-start.3 = (f32[4,4,64,1024]{3,2,1,0:T(8,128)}, f32[4,4,64,1024]{3,2,1,0:T(8,128)S(1)}, u32[]{:S(2)}) copy-start(f32[4,4,64,1024]{3,2,1,0:T(8,128)S(1)} %pad_add_fusion) | copy-start | bytes 12582916
  230.7 4.2 copy-start.20
  231.9 63.9 %collective-permute-start.2 = (f32[4,64,1024]{2,1,0:T(8,128)}, f32[4,64,1024]{2,1,0:T(8,128)S(1)}, u32[]{:S(2)}, u32[]{:S(2)}) collective-permute-start(f32[4,64,1024]{2,1,0:T(8,128)} %get-tuple-element.35), channel_id=1, source_target_pairs={{0,4},{4,8},{8,12},{12,16},{16,20},{20,24},{24,28},{1,5},{5,9},{9,... | collective-permute-start | bytes 3145736 | tf_op jit(solution)/shard_map/ppermute | solution.py:17
  233.5 62.2 %collective-permute-start.3 = (f32[4,64,1024]{2,1,0:T(8,128)S(1)}, f32[4,64,1024]{2,1,0:T(8,128)}, u32[]{:S(2)}, u32[]{:S(2)}) collective-permute-start(f32[4,64,1024]{2,1,0:T(8,128)S(1)} %get-tuple-element.36), channel_id=1, source_target_pairs={{4,0},{8,4},{12,8},{16,12},{20,16},{24,20},{28,24},{5,1},{9,5},{13... | collective-permute-start | bytes 3145736 | tf_op jit(solution)/shard_map/ppermute | solution.py:18
  235.0 4.4 copy-start.1
  235.0 4.4 copy-start.14
  295.7 4.0 copy-start.2
  302.1 2.4 copy-start.4
  302.1 3.5 copy-start.5
  313.2 222.5 %reduce-scatter.7.cloned.1.call-start = ((), (), s32[]{:S(2)}) async-start(), calls=%async_computation.7 | async-start | bytes 5242880
  313.5 4.8 copy-start.17
  318.3 5.7 %copy-start.18 = (bf16[4096,512]{1,0:T(8,128)(2,1)S(1)}, bf16[4096,512]{1,0:T(8,128)(2,1)}, u32[]{:S(2)}) copy-start(bf16[4096,512]{1,0:T(8,128)(2,1)} %param.12) | copy-start | bytes 12582916
  484.3 6.5 %copy-start.6 = (bf16[512,2048]{0,1:T(8,128)(2,1)S(1)}, bf16[512,2048]{0,1:T(8,128)(2,1)}, u32[]{:S(2)}) copy-start(bf16[512,2048]{0,1:T(8,128)(2,1)} %reduce-scatter.5.cloned.1.call-done) | copy-start | bytes 6291460
  (2 other events, 2.7 us)
Sparse Core Ops, SparseCore 0:
  9.8 55.3 all-gather.2
  67.1 52.6 all-gather.4
  122.8 59.7 all-reduce.8
  226.4 69.2 all-reduce.10
  313.3 167.8 reduce-scatter.4
  484.6 51.0 reduce-scatter.6
where the time goes:
time: 551 us; the launch traced here: 543 us
  waiting for transfers between devices  390 us (71%)
  matrix products  74.7 us (14%)
  local copies, waits for them, and re-layouts  35.6 us (6%)
  other arithmetic  20.1 us (4%)
  between operations  15.1 us (3%)
  starting transfers between devices  7.74 us (1%)
    reduce_scatter x1, waiting for transfers between devices, on_device(): lax.psum_scatter(whole_term.astype(jnp.bfloat16), 'seq', scatter_dimensio...  149 us
    all_gather x1, waiting for transfers between devices, on_device(): inputs = lax.all_gather(tokens, 'fsdp', axis=0, tiled=True)  54.5 us
    psum x1, waiting for transfers between devices, on_device(): glob_sum = lax.psum(grad_glob, 'seq')  52 us
    psum x1, waiting for transfers between devices, on_device(): global_kv = lax.psum(picked.astype(jnp.bfloat16), 'seq')  51.3 us
    unnamed x7, waiting for transfers between devices  44.7 us
    all_gather x1, waiting for transfers between devices, on_device(): grads_in = lax.all_gather(cotangent, 'fsdp', axis=0, tiled=True)  38 us
    dot_general x4, matrix products, contract_cols(): lax.dot_general(left, right, (((1,), (1,)), ((), ())), preferred_element_...  24 us
    dot_general x10, matrix products, product(): return jnp.einsum(form, left, right, preferred_element_type=jnp.float32)  16.4 us
  transfers between devices with their start and end apart: 10, of which 6 were waited for; matrix products, arithmetic and copies ran while one was open for 13% of the time, Pallas kernels for 0%

commit v1 on v0

v1 whole, which is shorter than its diff:
```python
import functools

import jax
import jax.numpy as jnp
from jax import lax
from jax.experimental import pallas as pl
from jax.experimental.pallas import tpu as pltpu
from jax.sharding import PartitionSpec as P

HDIM = 128
BLOCK = 64
LOW = -1e30
CORES = 2
TILE = 256
BF16 = jnp.bfloat16
F32 = jnp.float32


def swap(value, axis, mask):
    return lax.ppermute(value, axis, [(i, i ^ mask) for i in range(lax.axis_size(axis))])


def near_indices(count):
    return [1 << k for k in range(count.bit_length() - 1)]


def near_blocks(block, axis):
    return {r: swap(block, axis, r) for r in near_indices(lax.axis_size(axis))}


def far_blocks(halves, axis):
    count = lax.axis_size(axis)
    halves = dict(halves)
    for r in sorted(set(range(1, count)) - set(halves), key=lambda i: (bin(i).count("1"), i)):
        low, high = r & -r, 1 << (r.bit_length() - 1)
        halves[r] = (swap(halves[r ^ low][0], axis, low), swap(halves[r ^ high][1], axis, high))
    return halves


def cut(block):
    half = block.shape[0] // 2
    return block[:half], block[half:]


def phase(tree):
    return lax.optimization_barrier(tree)


class BlockScatter:
    def __init__(self, terms, axis):
        self.axis = axis
        self.terms = {r: [[piece] for piece in pieces] for r, pieces in terms.items()}

    def add(self, pieces):
        total = pieces[0]
        if len(pieces) > 1:
            total = pieces[0].astype(F32)
            for piece in pieces[1:]:
                total = total + piece.astype(F32)
        return total

    def send(self, weight):
        for r in [r for r in self.terms if bin(r).count("1") == weight]:
            ways = [r & -r, 1 << (r.bit_length() - 1)]
            for k, pieces in enumerate(self.terms[r]):
                value = swap(self.add(pieces).astype(BF16), self.axis, ways[k])
                there = self.terms[r ^ ways[k]]
                if weight > 2 or weight == 1:
                    there[k if weight > 2 else 0].append(value)
                else:
                    missing = jnp.zeros_like(value)
                    there[0].append(jnp.concatenate([value, missing] if k == 0 else [missing, value], 0))
            del self.terms[r]

    def collapse(self):
        for halves in self.terms.values():
            for pieces in halves:
                pieces[:] = [self.add(pieces).astype(BF16)]

    def own(self):
        return [pieces[0] for halves in self.terms.values() for pieces in halves]

    def put_own(self, values):
        for pieces in [pieces for halves in self.terms.values() for pieces in halves]:
            pieces[0] = values.pop(0)

    def total(self):
        return self.add(self.terms[0][0])


def halves_of(value, upper):
    half = value.shape[0] // 2
    mine = lax.dynamic_slice_in_dim(value, upper * half, half, 0)
    return mine, lax.dynamic_slice_in_dim(value, (1 - upper) * half, half, 0)


def sum_first(mine, other, chip):
    mine, other = halves_of(mine + swap(other, "seq", 1), chip & 1)
    return mine + swap(other, "seq", CORES)


def sum_second(value, chips):
    for k in range(1, chips.bit_length() - 1):
        last = swap(value, "seq", CORES << k)
        if k < chips.bit_length() - 2:
            value = value + last
    return value, last


def sum_third(value, chip):
    other = swap(value, "seq", CORES)
    return jnp.where(
        chip & 1 == 1, jnp.concatenate([other, value], 0), jnp.concatenate([value, other], 0)
    )


def sum_last(mine, core):
    other = swap(mine, "seq", 1)
    return jnp.where(core == 0, mine, other), jnp.where(core == 0, other, mine)


def shift_pairs(count, step):
    return [(i, i + step) for i in range(count) if 0 <= i + step < count]


def contract_rows(left, right):
    return lax.dot_general(left, right, (((0,), (0,)), ((), ())), preferred_element_type=F32)


def contract_cols(left, right):
    return lax.dot_general(left, right, (((1,), (1,)), ((), ())), preferred_element_type=F32)


RESIDENT = pl.BlockSpec(memory_space=pltpu.VMEM)


def resident(value):
    return pltpu.with_memory_space_constraint(value, pltpu.VMEM), RESIDENT


def fixed(shape):
    return pl.BlockSpec(shape, lambda *unused: (0,) * len(shape))


def call(kernel, grid, scalars, ins, outs, flops, limit=16, scratch=(), space=pltpu.HBM, free=()):
    return pl.pallas_call(
        kernel,
        grid_spec=pltpu.PrefetchScalarGridSpec(
            num_scalar_prefetch=1,
            grid=grid,
            in_specs=[spec for _, spec in ins],
            out_specs=[spec for _, _, spec in outs],
            scratch_shapes=scratch,
        ),
        out_shape=[space(shape, dtype) for shape, dtype, _ in outs],
        compiler_params=pltpu.CompilerParams(vmem_limit_bytes=limit << 20),
        cost_estimate=pl.CostEstimate(flops=flops >> 8, bytes_accessed=1024, transcendentals=0),
    )(
        scalars,
        *[a if k in free or spec is RESIDENT else pltpu.with_memory_space_constraint(a, pltpu.HBM) for k, (a, spec) in enumerate(ins)],
    )


def accumulate(total_ref, term):
    @pl.when(pl.program_id(0) == 0)
    def _():
        total_ref[...] = term

    @pl.when(pl.program_id(0) > 0)
    def _():
        total_ref[...] += term


def fill(parts, flat_ref):
    start = 0
    for part in parts:
        flat_ref[start : start + part.shape[0]] = part[...]
        start += part.shape[0]


def keys_kernel(tiles, docs, core_ref, *refs):
    *parts, sel_ref, wk_ref, wv_ref = refs[:-7]
    k_ref, v_ref, first_ref, last_ref, mine_ref, other_ref, flat_ref = refs[-7:]
    step, core = pl.program_id(0), core_ref[0]

    @pl.when(step == 0)
    def _():
        fill(parts, flat_ref)

    def emit(weight_ref, out_ref, owner):
        out = jnp.dot(flat_ref[...], weight_ref[...], preferred_element_type=F32).astype(BF16)
        out_ref[...] = out
        rows = out.shape[0] // docs
        globs = sel_ref.shape[0] // docs
        picked = []
        for doc in range(docs):
            part = out[doc * rows : (doc + 1) * rows]
            first_ref[doc * BLOCK : (doc + 1) * BLOCK] = part[:BLOCK]
            last_ref[doc * BLOCK : (doc + 1) * BLOCK] = part[rows - BLOCK :]
            chosen = sel_ref[doc * globs : (doc + 1) * globs]
            picked.append(jnp.dot(chosen, part, preferred_element_type=F32).astype(BF16))

        @pl.when(core == owner)
        def _():
            for doc in range(docs):
                mine_ref[doc * globs : (doc + 1) * globs] = picked[doc]

        @pl.when(core != owner)
        def _():
            for doc in range(docs):
                other_ref[doc * globs : (doc + 1) * globs] = picked[doc]

    @pl.when(step < tiles)
    def _():
        emit(wk_ref, k_ref, 0)

    @pl.when(step >= tiles)
    def _():
        emit(wv_ref, v_ref, 1)


def project_keys(parts, selector, w_key, w_value, core, docs):
    rows = sum(p.shape[0] for p in parts)
    depth, width = w_key.shape
    tile = min(TILE, width // 2)
    tiles = width // tile
    low = lambda i, *_: (0, jnp.minimum(i, tiles - 1))
    high = lambda i, *_: (0, jnp.maximum(i - tiles, 0))
    each = lambda i, *_: (0, i)
    share = lambda owner: lambda i, c: (
        0, jnp.clip(i - tiles * jnp.where(c[0] == owner, 0, 1), 0, tiles - 1)
    )
    globs = selector.shape[0]
    edge = docs * BLOCK
    return call(
        functools.partial(keys_kernel, tiles, docs),
        (2 * tiles,),
        core.reshape(1),
        [resident(p) for p in parts]
        + [(selector, fixed(selector.shape))]
        + [(w_key, pl.BlockSpec((depth, tile), low)), (w_value, pl.BlockSpec((depth, tile), high))],
        [
            ((rows, width), BF16, pl.BlockSpec((rows, tile), low)),
            ((rows, width), BF16, pl.BlockSpec((rows, tile), high)),
            ((edge, 2 * width), BF16, pl.BlockSpec((edge, tile), each)),
            ((edge, 2 * width), BF16, pl.BlockSpec((edge, tile), each)),
            ((globs, width), BF16, pl.BlockSpec((globs, tile), share(0))),
            ((globs, width), BF16, pl.BlockSpec((globs, tile), share(1))),
        ],
        4 * rows * depth * width,
        limit=(rows + 4 * tile) * depth * 2 // 2**20 + 8,
        scratch=[pltpu.VMEM((rows, depth), BF16)],
    )


def project_kernel(flip, tiles, slices, core_ref, *refs):
    *parts, w_ref = refs[:-4]
    flat_ref, send_ref, out_ref, whole_ref = refs[-4:]
    step, core = pl.program_id(0), core_ref[0]
    size = whole_ref.shape[1] // slices

    @pl.when(step == 0)
    def _():
        fill(parts, whole_ref)

    for index in range(tiles):

        @pl.when(step == index)
        def _(index=index):
            if flip:
                out_ref[...] = contract_cols(whole_ref[...], w_ref[...]).astype(BF16)
            else:
                out = jnp.dot(whole_ref[...], w_ref[...], preferred_element_type=F32)
                out_ref[...] = out.astype(BF16)
            wide = flat_ref.shape[1]
            flat_ref[...] = whole_ref[:, index * wide : (index + 1) * wide]
            for k in range(slices // CORES // tiles):
                shard = CORES * (index * (slices // CORES // tiles) + k)
                begin = pl.multiple_of((shard + CORES - 1 - core) * size, size)
                send_ref[:, k * size : (k + 1) * size] = whole_ref[:, pl.ds(begin, size)]


def project(parts, weight, core, slices, flip):
    rows = sum(p.shape[0] for p in parts)
    depth, width = weight.shape[::-1] if flip else weight.shape
    tile = min(TILE, width // 2)
    tiles = width // tile
    each = lambda i, *_: (0, i)
    return call(
        functools.partial(project_kernel, flip, tiles, slices),
        (tiles,),
        core.reshape(1),
        [(p, fixed(p.shape)) if flip else resident(p) for p in parts]
        + [(weight, pl.BlockSpec((tile, depth), lambda i, *_: (i, 0)) if flip else pl.BlockSpec((depth, tile), each))],
        [
            ((rows, depth), BF16, pl.BlockSpec((rows, depth // tiles), each)),
            ((rows, depth // CORES), BF16, pl.BlockSpec((rows, depth // CORES // tiles), each)),
            ((rows, width), BF16, pl.BlockSpec((rows, tile), each)),
        ],
        2 * rows * depth * width,
        limit=((rows * (tiles + 3) // tiles + 2 * tile) + 2 * rows * flip) * depth * 2 // 2**20 + 5,
        scratch=[pltpu.VMEM((rows, depth), BF16)],
    )


def key_mask(flags_ref, doc, rows, total):
    row_block = lax.broadcasted_iota(jnp.int32, (rows, total), 0) // BLOCK
    col = lax.broadcasted_iota(jnp.int32, (rows, total), 1)
    offset = col // BLOCK - row_block
    seen = (offset == 1) | (col >= rows + 2 * BLOCK)
    window = col < rows + 2 * BLOCK
    for block in range(rows // BLOCK):
        here = (row_block == block) & window
        before = flags_ref[doc, 2 * block] == 1
        past = flags_ref[doc, 2 * block + 1] == 1
        seen = seen | (here & (offset == 0) & before) | (here & (offset == 2) & past)
    return seen


def joined(before_ref, own_ref, after_ref, glob_ref, head, shift):
    cols = slice(head * HDIM, (head + 1) * HDIM)
    side = slice(shift + head * HDIM, shift + (head + 1) * HDIM)
    return jnp.concatenate(
        [before_ref[:, side], own_ref[:, cols], after_ref[:, side], glob_ref[:, cols]], 0
    )


def attention_kernel(
    flags_ref, q_ref, k_ref, v_ref, before_ref, after_ref, gk_ref, gv_ref, do_ref,
    ctx_ref, dq_ref, dk_ref, dv_ref, dbefore_ref, dafter_ref, mine_ref, other_ref,
):
    rows, width = q_ref.shape
    total = rows + 2 * BLOCK + gk_ref.shape[0]
    doc = pl.program_id(0)
    seen = key_mask(flags_ref, doc, rows, total)
    first_core = flags_ref[doc, 2 * (rows // BLOCK)] == 0
    heads = range(width // HDIM)
    cols = [slice(head * HDIM, (head + 1) * HDIM) for head in heads]
    keys = [joined(before_ref, k_ref, after_ref, gk_ref, head, 0) for head in heads]
    values = [joined(before_ref, v_ref, after_ref, gv_ref, head, width) for head in heads]
    scores = [contract_cols(q_ref[:, cols[h]], keys[h]) * HDIM**-0.5 for h in heads]
    dweights = [contract_cols(do_ref[:, cols[h]], values[h]) for h in heads]
    scores = [jnp.where(seen, s, LOW) for s in scores]
    tops = [s.max(-1, keepdims=True) for s in scores]
    grown = [jnp.exp(scores[h] - tops[h]) for h in heads]
    sums = [g.sum(-1, keepdims=True) for g in grown]
    weights = [grown[h] / sums[h] for h in heads]
    deltas = [(weights[h] * dweights[h]).sum(-1, keepdims=True) for h in heads]
    weights_b = [w.astype(BF16) for w in weights]
    for h in heads:
        ctx_ref[:, cols[h]] = jnp.dot(weights_b[h], values[h], preferred_element_type=F32).astype(BF16)
    dvalues = [contract_rows(weights_b[h], do_ref[:, cols[h]]) for h in heads]
    dscores = [
        (weights[h] * (dweights[h] - deltas[h]) * HDIM**-0.5).astype(BF16) for h in heads
    ]
    for h in heads:
        dq_ref[:, cols[h]] = jnp.dot(dscores[h], keys[h], preferred_element_type=F32).astype(BF16)
    dkeys = [contract_rows(dscores[h], q_ref[:, cols[h]]) for h in heads]
    for h in heads:
        for own_ref, shift, grads in ((dk_ref, 0, dkeys[h]), (dv_ref, width, dvalues[h])):
            side = slice(shift + h * HDIM, shift + (h + 1) * HDIM)
            own_ref[:, cols[h]] = grads[BLOCK : rows + BLOCK]
            dbefore_ref[:, side] = grads[:BLOCK].astype(BF16)
            dafter_ref[:, side] = grads[rows + BLOCK : rows + 2 * BLOCK].astype(BF16)
        gk, gv = dkeys[h][rows + 2 * BLOCK :], dvalues[h][rows + 2 * BLOCK :]
        mine_ref[:, cols[h]] = jnp.where(first_core, gk, gv).astype(BF16)
        other_ref[:, cols[h]] = jnp.where(first_core, gv, gk).astype(BF16)


def by_doc(rows, width):
    return pl.BlockSpec((rows, width), lambda doc, *unused: (doc, 0))


def attention(kernel, docs, flags, operands, out_rows, flops, free):
    return call(
        kernel,
        (docs,),
        flags,
        [(a, by_doc(a.shape[0] // docs, a.shape[1])) for a in operands],
        [((docs * rows, width), dtype, by_doc(rows, width)) for rows, width, dtype in out_rows],
        flops,
        free=free,
    )


def finish_kernel(
    core_ref, dq_ref, dk_ref, dv_ref, ctx_ref, before_ref, after_ref, keys_ref, values_ref
):
    rows, width = dk_ref.shape
    keys_ref[:, :width] = dq_ref[...]
    values_ref[:, :width] = ctx_ref[...]
    cols = slice(width, 2 * width)
    for own_ref, shift, out_ref in ((dk_ref, 0, keys_ref), (dv_ref, width, values_ref)):
        side = slice(shift, shift + width)
        out_ref[:BLOCK, cols] = (own_ref[:BLOCK] + before_ref[:, side].astype(F32)).astype(BF16)
        if rows > 2 * BLOCK:
            out_ref[BLOCK : rows - BLOCK, cols] = own_ref[BLOCK : rows - BLOCK].astype(BF16)
        out_ref[rows - BLOCK :, cols] = (own_ref[rows - BLOCK :] + after_ref[:, side].astype(F32)).astype(BF16)


def whole_kernel(
    core_ref, dk_ref, dv_ref, before_ref, after_ref, gk_ref, gv_ref, sel_ref, k_ref, v_ref
):
    rows, width = dk_ref.shape
    for own_ref, glob_ref, shift, out_ref in ((dk_ref, gk_ref, 0, k_ref), (dv_ref, gv_ref, width, v_ref)):
        total = own_ref[...] + contract_rows(sel_ref[...], glob_ref[...])
        side = slice(shift, shift + width)
        out_ref[:BLOCK] = (total[:BLOCK] + before_ref[:, side].astype(F32)).astype(BF16)
        if rows > 2 * BLOCK:
            out_ref[BLOCK : rows - BLOCK] = total[BLOCK : rows - BLOCK].astype(BF16)
        out_ref[rows - BLOCK :] = (total[rows - BLOCK :] + after_ref[:, side].astype(F32)).astype(BF16)


def transposed(value):
    return value.astype(F32).T.astype(value.dtype)


def terms_kernel(core_ref, c_ref, csib_ref, x_ref, xsib_ref, g_ref, gsib_ref, out_ref, turned_ref):
    rows, width = g_ref.shape[0], g_ref.shape[1] // 2
    size = x_ref.shape[1]

    @pl.when(pl.program_id(0) == 0)
    def _():
        turned_ref[:, :rows] = transposed(g_ref[...])
        turned_ref[:, rows:] = transposed(gsib_ref[...])

    for k, (own_ref, sib_ref) in enumerate(((c_ref, csib_ref), (x_ref, xsib_ref))):
        both = jnp.concatenate([own_ref[...], sib_ref[...]], 0)
        out = jnp.dot(turned_ref[k * width : (k + 1) * width], both, preferred_element_type=F32)
        out_ref[0, :, k * size : (k + 1) * size] = out.astype(BF16)


def chip_terms(cots, tokens, grads, core, slices):
    rows, depth = cots[0].shape
    width = grads.shape[1] // 2
    size, chips = depth // slices, slices // CORES
    own = pl.BlockSpec((rows, size), lambda z, c: (0, CORES * z + c[0]))
    other = pl.BlockSpec((rows, size), lambda z, c: (0, z))
    return call(
        terms_kernel,
        (chips,),
        core.reshape(1),
        [
            (cots[0], own),
            (cots[1], other),
            (tokens[0], own),
            (tokens[1], other),
            (grads, fixed(grads.shape)),
            (swap(grads, "seq", 1), fixed(grads.shape)),
        ],
        [((chips, width, 2 * size), BF16, pl.BlockSpec((1, width, 2 * size), lambda z, c: (z, 0, 0)))],
        8 * rows * size * chips * width,
        limit=24,
        scratch=[pltpu.VMEM((2 * width, 2 * rows), BF16)],
    )[0]


def line_schedule(count):
    return [
        {
            c: ("all", c - step) if step <= c else ("sum", count + c - step)
            for c in range(count - 1)
        }
        for step in range(count)
    ]


def pieces_kernel(count, table_ref, right_ref, left_ref, *refs):
    for way, (own_ref, out_ref) in enumerate(((right_ref, refs[-2]), (left_ref, refs[-1]))):
        is_sum, begins = table_ref[3 * way + 1] == 1, table_ref[3 * way + 2] == 1
        begin = 0
        for came_ref in refs[way * count : (way + 1) * count]:
            here = slice(begin, begin + came_ref.shape[1])
            begin += came_ref.shape[1]
            own, came = own_ref[0, :, here], came_ref[...]
            added = (own.astype(F32) + came.astype(F32)).astype(BF16)
            out_ref[:, here] = jnp.where(is_sum, jnp.where(begins, own, added), came)


def lookup(place, values):
    result = jnp.int32(values[0])
    for k, value in enumerate(values[1:], 1):
        result = jnp.where(place == k, jnp.int32(value), result)
    return result


class Line:
    def __init__(self, shape, chip, chips):
        self.partial, self.chip, self.chips, self.shape = None, chip, chips, shape
        self.schedule = line_schedule(chips)
        self.values, self.firsts, self.received = [], [], []

    def begin(self, value):
        self.values.append(value)
        self.firsts.append(self.move((value, value)))

    def join(self):
        self.rows, self.wide = self.values[0].shape[0], sum(v.shape[1] for v in self.values)
        self.size = tuple(max(a, b) for a, b in zip((self.rows, self.wide), self.shape))
        self.received.append(tuple(self.fit(jnp.concatenate(way, 1)) for way in zip(*self.firsts)))

    def fit(self, value):
        missing = [(0, want - have) for want, have in zip(self.size, value.shape)]
        return jnp.pad(value, missing) if any(m for _, m in missing) else value

    def place(self, sign):
        return self.chip if sign > 0 else self.chips - 1 - self.chip

    def pieces(self):
        chosen, pieces, table = self.schedule[len(self.received)], [], []
        count = self.chips
        plain = len(self.firsts) > 1 and len(self.received) == 1 and self.size == self.shape == (self.rows, self.wide)
        for way, sign in enumerate((1, -1)):
            place = self.place(sign)
            sums = [int(chosen.get(c, ("", 0))[0] == "sum") for c in range(count)]
            which = [chosen.get(c, ("", c))[1] for c in range(count)]
            to = lookup(place, which)
            to = to if sign > 0 else count - 1 - to
            if plain:
                table += [to, lookup(place, sums), (place == 0).astype(jnp.int32)]
                continue
            own = self.fit(lax.dynamic_index_in_dim(self.partial, to, 0, keepdims=False))
            before = self.received[-1][way]
            added = (own.astype(F32) + before.astype(F32)).astype(BF16)
            pieces.append(jnp.where(lookup(place, sums) == 1, jnp.where(place == 0, own, added), before))
        if not plain:
            return pieces
        arrived = [list(way) for way in zip(*self.firsts)]
        rows, wide = self.size
        part = rows // 4
        return call(
            functools.partial(pieces_kernel, len(arrived[0])),
            (4,),
            jnp.stack(table),
            [(self.partial, pl.BlockSpec((1, part, wide), lambda i, t, at=at: (t[at], i, 0))) for at in (0, 3)]
            + [(a, pl.BlockSpec((part, a.shape[1]), lambda i, *_: (i, 0))) for way in arrived for a in way],
            [((rows, wide), BF16, pl.BlockSpec((part, wide), lambda i, *_: (i, 0)))] * 2,
            0,
            space=jax.ShapeDtypeStruct,
            free=range(2, 8),
        )

    def move(self, pieces):
        count, got = self.chips, []
        for piece, sign in zip(pieces, (1, -1)):
            pairs = [
                (c * CORES + b, (c + sign) * CORES + b)
                for c in (range(count - 1) if sign > 0 else range(count - 1, 0, -1))
                for b in range(CORES)
            ]
            got.append(lax.ppermute(piece, "seq", pairs))
        return tuple(got)

    def send(self, pieces):
        self.received.append(self.move(pieces))

    def step(self):
        self.send(self.pieces())

    def gathered(self, columns, sums, positions, core):
        rows, wide = self.rows, self.wide
        slots, grads = [jnp.int32(0)], [self.values]
        for t in range(self.chips - 1):
            for way, sign in enumerate((1, -1)):
                values = [-1] * self.chips
                for c, (kind, which) in self.schedule[t].items():
                    if kind == "all":
                        values[c + 1] = (sign * (c + 1 - which)) % self.chips
                slots.append(lookup(self.place(sign), values))
                if t:
                    grads.append([self.received[t][way][:rows, :wide]])
                else:
                    grads.append([first[way] for first in self.firsts])
        height, width = columns[0].shape[1], wide // 2
        size = height // CORES
        once = lambda a: (a, pl.BlockSpec(a.shape, lambda *_: (0,) * a.ndim, pipeline_mode=pl.Buffered(1)))
        return call(
            functools.partial(gathered_kernel, len(columns), [len(g) for g in grads]),
            (1,),
            jnp.stack(slots + [core, self.chip]),
            [once(a) for a in columns + list(sums) + [positions] + sum(grads, [])],
            [
                ((size, 3 * width), F32, fixed((size, 3 * width))),
            ]
            + [((size, width), BF16, fixed((size, width)))] * 3,
            4 * height * width * len(grads) * rows,
            limit=44,
            scratch=[pltpu.VMEM((height, 3 * width), F32)],
        )


def final_kernel(
    chip_ref, terms_ref, right_ref, left_ref, mine_ref, *refs
):
    others, (q_ref, k_ref, v_ref, o_ref) = refs[:3], refs[3:]
    width, size = q_ref.shape[1], o_ref.shape[1]
    rows, wide = terms_ref.shape[1:]
    summed = terms_ref[0].astype(F32)
    summed += right_ref[:rows, :wide].astype(F32)
    summed += left_ref[:rows, :wide].astype(F32)
    o_ref[...] = summed[:, :size]
    q_ref[...] = mine_ref[:, :width] + others[0][...].astype(F32)
    k_ref[...] = mine_ref[:, width : 2 * width] + others[1][...].astype(F32)
    v_ref[...] = mine_ref[:, 2 * width :] + others[2][...].astype(F32) + summed[:, size:].T


def final_sums(line, mine, others, width):
    _, rows, wide = line.partial.shape
    size = mine.shape[0]
    return call(
        final_kernel,
        (1,),
        line.chip.reshape(1),
        [(line.partial, pl.BlockSpec((1, rows, wide), lambda i, c: (c[0], 0, 0)))]
        + [(a, fixed(a.shape)) for a in (*line.received[-1], mine, *others)],
        [((size, width), F32, fixed((size, width)))] * 3 + [((rows, size), F32, fixed((rows, size)))],
        0,
        limit=32,
        free=range(1, 7),
    )


def columns_to_chips(block, chip, chips):
    turned = block.T
    size = turned.shape[0] // chips
    pieces = []
    for s in range(chips):
        piece = lax.dynamic_slice_in_dim(turned, lax.rem(chip + s, chips) * size, size, 0)
        if s:
            pairs = [
                (c * CORES + b, (c + s) % chips * CORES + b) for c in range(chips) for b in range(CORES)
            ]
            piece = lax.ppermute(piece, "seq", pairs)
        pieces.append(piece)
    return pieces


def gathered_kernel(docs, groups, slots_ref, *refs):
    x_refs, (gk_ref, gv_ref, positions_ref), g_refs = refs[:docs], refs[docs : docs + 3], refs[docs + 3 : -5]
    mine_ref, *other_refs, total_ref = refs[-5:]
    width = gk_ref.shape[1]
    sent = 2 * width
    chips, _, rows = x_refs[0].shape
    core, chip = slots_ref[len(groups)], slots_ref[len(groups) + 1]

    def add(slot, group, first):
        x = jnp.concatenate([x_ref[slot] for x_ref in x_refs], 1)
        begin = 0
        for g_ref in group:
            here = slice(begin, begin + g_ref.shape[1])
            term = jnp.dot(x, g_ref[...], preferred_element_type=F32)
            total_ref[:, here] = term if first else total_ref[:, here] + term
            begin += g_ref.shape[1]

    begin = 0
    for k, count in enumerate(groups):
        group = g_refs[begin : begin + count]
        begin += count
        if k == 0:
            add(0, group, True)
            continue

        @pl.when(slots_ref[k] >= 0)
        def _(k=k, group=group):
            add(slots_ref[k], group, False)

    globs = gk_ref.shape[0] // docs
    chosen = []
    for doc in range(docs):
        picked = None
        for slot in range(chips):
            begin = (lax.rem(chip + chips - slot, chips) * CORES + core) * rows
            place = begin + lax.broadcasted_iota(jnp.int32, (rows, globs), 0)
            onehot = (place == positions_ref[doc]).astype(F32).astype(BF16)
            part = jnp.dot(x_refs[doc][slot], onehot, preferred_element_type=F32)
            picked = part if picked is None else picked + part
        chosen.append(picked.astype(BF16))
    chosen = jnp.concatenate(chosen, 1)
    total_ref[:, sent - width : sent] += jnp.dot(chosen, gk_ref[...], preferred_element_type=F32)
    total_ref[:, sent:] = jnp.dot(chosen, gv_ref[...], preferred_element_type=F32)

    size = mine_ref.shape[0]
    mine_ref[...] = total_ref[pl.ds(pl.multiple_of(core * size, size), size)]
    other = total_ref[pl.ds(pl.multiple_of((CORES - 1 - core) * size, size), size)]
    for k, other_ref in enumerate(other_refs):
        other_ref[...] = other[:, k * width : (k + 1) * width].astype(BF16)


def tokens_kernel(places, core_ref, q_ref, k_ref, v_ref, wq_ref, wk_ref, wv_ref, *out_refs):
    total = None
    for g_ref, w_ref in ((q_ref, wq_ref), (k_ref, wk_ref), (v_ref, wv_ref)):
        term = contract_cols(w_ref[...], g_ref[...])
        total = term if total is None else total + term
    total = total.T.astype(BF16)
    for (begin, count), out_ref in zip(places, out_refs):
        out_ref[...] = total[begin : begin + count]


def token_terms(docs, rows, grads, weights, core):
    depth, width = weights[0].shape
    tile = 512
    places = []
    for r in range(docs):
        halves = 2 if bin(r).count("1") > 1 else 1
        places += [(r * rows + k * rows // halves, rows // halves) for k in range(halves)]
    pieces = call(
        functools.partial(tokens_kernel, places),
        (depth // tile,),
        core.reshape(1),
        [(g, fixed(g.shape)) for g in grads]
        + [(w, pl.BlockSpec((tile, width), lambda i, *_: (i, 0))) for w in weights],
        [((count, depth), BF16, pl.BlockSpec((count, tile), lambda i, *_: (0, i))) for _, count in places],
        6 * docs * rows * depth * width,
        limit=24,
    )
    terms = {r: [] for r in range(docs)}
    for (begin, _), piece in zip(places, pieces):
        terms[begin // rows].append(piece)
    return terms


def on_device(tokens, cotangent, w_query, w_key, w_value, w_output, global_pos, pattern):
    docs = lax.axis_size("fsdp")
    n_seq = lax.axis_size("seq")
    seq = lax.axis_index("seq")
    core, chip, chips = lax.rem(seq, CORES), lax.div(seq, CORES), n_seq // CORES
    rows, model_width = tokens.shape[1:]
    width = w_query.shape[1]
    block_count = rows // BLOCK
    order = lax.axis_index("fsdp") ^ jnp.arange(docs, dtype=jnp.int32)
    global_pos = jnp.take(global_pos, order, axis=0)
    pattern = jnp.take(pattern, order, axis=0)
    globs = global_pos.shape[1]

    index = seq * block_count + jnp.arange(block_count, dtype=jnp.int32)
    inside = jnp.stack([index > 0, index < block_count * n_seq - 1], -1)
    flags = ((pattern == 1) & inside[None]).astype(jnp.int32).reshape(docs, 2 * block_count)
    flags = jnp.concatenate([flags, jnp.broadcast_to(core, (docs, 1))], 1)
    selector = (
        (global_pos[:, :, None] - seq * rows == jnp.arange(rows, dtype=jnp.int32)[None, None, :])
        .astype(BF16)
        .reshape(docs * globs, rows)
    )

    block, cot = tokens[0], cotangent[0]
    pieces = columns_to_chips(block, chip, chips)
    near, selector, flags = phase((near_blocks(block, "fsdp"), selector, flags))
    whole = {0: block, **near}
    far = far_blocks({r: cut(v) for r, v in whole.items()}, "fsdp")
    parts = [p for r in range(docs) for p in ([whole[r]] if r in whole else far[r])]
    parts, cot_halves, pieces = phase((parts, cut(cot), pieces))

    near_a = near_blocks(cot_halves[0], "fsdp")
    keys, values, first, last, mine, other = project_keys(
        parts, selector, w_key, w_value, core, docs
    )
    keys, values, first, last, mine, other, near_a, cot_b, parts, pieces = phase(
        (keys, values, first, last, mine, other, near_a, cot_halves[1], parts, pieces)
    )

    near_b = near_blocks(cot_b, "fsdp")
    glob = sum_first(mine, other, chip)
    flat, for_sibling, query = project(parts, w_query, core, n_seq, False)
    glob, near_b, flat, query, for_sibling, first, last, pieces = phase(
        (glob, near_b, flat, query, for_sibling, first, last, pieces)
    )
    halves = {0: (cot_halves[0], cot_b)}
    halves.update({r: (near_a[r], near_b[r]) for r in near_a})
    far = far_blocks(halves, "fsdp")
    glob = sum(sum_second(glob, chips))
    columns = jnp.stack(pieces)
    glob, far, first, last, for_sibling, columns = phase((glob, far, first, last, for_sibling, columns))
    glob = sum_third(glob, chip)
    past = lax.ppermute(first, "seq", shift_pairs(n_seq, -1))
    before = lax.ppermute(last, "seq", shift_pairs(n_seq, 1))
    cot_parts = [cot] + [p for r in range(1, docs) for p in far[r]]
    grads_flat, grads_for_sibling, grad_ctx = project(cot_parts, w_output, core, n_seq, True)
    glob, grads_flat, grads_for_sibling, grad_ctx, columns, for_sibling, past, before = phase(
        (glob, grads_flat, grads_for_sibling, grad_ctx, columns, for_sibling, past, before)
    )
    glob_k, glob_v = sum_last(glob, core)
    glob_k, glob_v, grads_for_sibling, for_sibling = phase(
        (glob_k, glob_v, grads_for_sibling, for_sibling)
    )
    grads_sibling = swap(grads_for_sibling, "seq", 1)
    tokens_sibling = swap(for_sibling, "seq", 1)

    near_columns = near_blocks(columns, "fsdp")
    context, grad_q, dkey, dvalue, dbefore, dafter, dmine, dother = attention(
        attention_kernel,
        docs,
        flags,
        [query, keys, values, before, past, glob_k, glob_v, grad_ctx],
        [
            (rows, width, BF16),
            (rows, width, BF16),
            (rows, width, F32),
            (rows, width, F32),
            (BLOCK, 2 * width, BF16),
            (BLOCK, 2 * width, BF16),
            (globs, width, BF16),
            (globs, width, BF16),
        ],
        14 * docs * rows * (rows + 2 * BLOCK + globs) * width,
        free=(3, 4, 5, 6),
    )

    (context, grad_q, dkey, dvalue, dbefore, dafter, dmine, dother), columns, grads_sibling, tokens_sibling = phase(
        ((context, grad_q, dkey, dvalue, dbefore, dafter, dmine, dother), columns, grads_sibling, tokens_sibling)
    )

    line = Line((width, 2 * model_width // n_seq), chip, chips)
    kept, given = halves_of(dmine + swap(dother, "seq", 1), chip & 1)
    kept, given, dbefore, dafter, grad_q = phase((kept, given, dbefore, dafter, grad_q))
    given = swap(given, "seq", CORES)
    from_after = lax.ppermute(dbefore, "seq", shift_pairs(n_seq, -1))
    from_before = lax.ppermute(dafter, "seq", shift_pairs(n_seq, 1))
    dglob, context = phase((kept + given, context))
    dglob, came = sum_second(dglob, chips)
    to_gather, to_scatter = call(
        finish_kernel,
        (docs,),
        core.reshape(1),
        [
            (a, by_doc(a.shape[0] // docs, a.shape[1]))
            for a in (grad_q, dkey, dvalue, context, from_before, from_after)
        ],
        [((docs * rows, 2 * width), BF16, by_doc(rows, 2 * width))] * 2,
        4 * docs * rows * globs * width,
        free=(4, 5),
    )
    to_gather, to_scatter, columns, near_columns, came = phase(
        (to_gather, to_scatter, columns, near_columns, came)
    )
    dglob = dglob + came

    line.begin(to_gather)
    line.partial = chip_terms((grads_flat, grads_sibling), (flat, tokens_sibling), to_scatter, core, n_seq)
    line.firsts, line.partial, dglob = phase((line.firsts, line.partial, dglob))
    line.join()
    line.step()
    dglob = sum_third(dglob, chip)
    whole = {0: columns, **near_columns}
    far = far_blocks({r: cut(v) for r, v in whole.items()}, "fsdp")
    sums = sum_last(dglob, core)
    grad_k, grad_v = call(
        whole_kernel,
        (docs,),
        core.reshape(1),
        [
            (a, by_doc(a.shape[0] // docs, a.shape[1]))
            for a in (dkey, dvalue, from_before, from_after, *sums, selector)
        ],
        [((docs * rows, width), BF16, by_doc(rows, width))] * 2,
        4 * docs * rows * globs * width,
        free=(4, 5),
    )
    terms = token_terms(docs, rows, (grad_q, grad_k, grad_v), (w_query, w_key, w_value), core)
    line.received, sums, far, whole, terms = phase((line.received, sums, far, whole, terms))
    scatter, bits = BlockScatter(terms, "fsdp"), docs.bit_length() - 1
    pieces, far, own_terms = phase((line.pieces(), far, scatter.own()))
    scatter.put_own(own_terms)
    line.send(pieces)
    columns = [whole[r] if r in whole else jnp.concatenate(far[r], 0) for r in range(docs)]
    scatter.send(bits)
    scatter.collapse()
    line.received, sums, columns, scatter.terms = phase((line.received, sums, columns, scatter.terms))
    while len(line.received) < len(line.schedule) - 1:
        line.step()
    pieces, sums, columns, own_terms = phase((line.pieces(), sums, columns, scatter.own()))
    scatter.put_own(own_terms)
    line.send(pieces)
    for weight in range(bits - 1, 0, -1):
        scatter.send(weight)
    mine, *others = line.gathered(columns, sums, global_pos[:, None, :], core)
    grad_tokens, others = phase((scatter.total().astype(BF16)[None], others))
    others = [swap(other, "seq", 1) for other in others]
    line.received, mine, others = phase((line.received, mine, others))
    grad_query, grad_key, grad_value, grad_output = final_sums(line, mine, others, width)
    return (grad_tokens, grad_query, grad_key, grad_value, grad_output)


def solution(mesh):
    in_specs = (
        P("fsdp", "seq", None),
        P("fsdp", "seq", None),
        P(None, "fsdp"),
        P(None, "fsdp"),
        P(None, "fsdp"),
        P("fsdp", None),
        P(),
        P(None, "seq", None),
    )
    out_specs = (
        P("fsdp", "seq", None),
        P("seq", "fsdp"),
        P("seq", "fsdp"),
        P("seq", "fsdp"),
        P("fsdp", "seq"),
    )
    return jax.shard_map(
        on_device, mesh=mesh, in_specs=in_specs, out_specs=out_specs, check_vma=False
    )
```

time: 551 us -> 285 us (0.52); the launches traced: 543 us -> 284 us
  waiting for transfers between devices: 390 us -> 89.3 us
  Pallas kernels: 0 us -> 82.3 us
  matrix products: 74.7 us -> 0 us
  starting transfers between devices: 7.74 us -> 70.8 us
  local copies, waits for them, and re-layouts: 35.6 us -> 15.8 us
  between operations: 15.1 us -> 1.3 us
    reduce_scatter x1 -> x0, waiting for transfers between devices: 149 us -> none  [on_device(): lax.psum_scatter(whole_term.astype(jnp.bfloat16), 'seq', scatter_dimensio...]
    psum x2 -> x0, waiting for transfers between devices: 103 us -> none  [the longest x1 52 us: on_device(): glob_sum = lax.psum(grad_glob, 'seq')]
    all_gather x2 -> x0, waiting for transfers between devices: 92.5 us -> none  [the longest x1 54.5 us: on_device(): inputs = lax.all_gather(tokens, 'fsdp', axis=0, tiled=True)]
    ppermute x4 -> x49, waiting for transfers between devices: 0.01 us -> 89.3 us  [the longest x34 55.4 us: swap(): lax.ppermute(value, axis, [(i, i ^ mask) for i in range(lax.axis_size(axi...]
    pallas_call x0 -> x10, Pallas kernels: none -> 82.3 us  [call(): pl.pallas_call(kernel, grid_spec=pltpu.PrefetchScalarGridSpec(num_scalar_...]
    dot_general x23 -> x0, matrix products: 73.7 us -> none  [the longest x4 24 us: contract_cols(): lax.dot_general(left, right, (((1,), (1,)), ((), ())), preferred_element_...]
    ppermute x4 -> x49, starting transfers between devices: 7.04 us -> 70.8 us  [the longest x34 38.9 us: swap(): lax.ppermute(value, axis, [(i, i ^ mask) for i in range(lax.axis_size(axi...]
    unnamed x7 -> x0, waiting for transfers between devices: 44.7 us -> none
  transfers between devices with their start and end apart: 10 -> 49, of which waited for: 6 -> 20; matrix products, arithmetic and copies ran while one was open for 13% -> 12% of each run, Pallas kernels for 0% -> 28%
where the time goes in v1:
time: 285 us; the launch traced here: 284 us
  waiting for transfers between devices  89.3 us (31%)
  Pallas kernels  82.3 us (29%)
  starting transfers between devices  70.8 us (25%)
  other arithmetic  24.2 us (8%)
  local copies, waits for them, and re-layouts  15.8 us (6%)
    pallas_call x10, Pallas kernels, call(): pl.pallas_call(kernel, grid_spec=pltpu.PrefetchScalarGridSpec(num_scalar_...  82.3 us
    ppermute x34, waiting for transfers between devices, swap(): lax.ppermute(value, axis, [(i, i ^ mask) for i in range(lax.axis_size(axi...  55.4 us
    ppermute x34, starting transfers between devices, swap(): lax.ppermute(value, axis, [(i, i ^ mask) for i in range(lax.axis_size(axi...  38.9 us
    ppermute x8, waiting for transfers between devices, move(): got.append(lax.ppermute(piece, 'seq', pairs))  33.9 us
    ppermute x8, starting transfers between devices, move(): got.append(lax.ppermute(piece, 'seq', pairs))  18.8 us
    select_n x3, other arithmetic, pieces(): jnp.where(lookup(place, sums) == 1, jnp.where(place == 0, own, added), be...  6.75 us
  transfers between devices with their start and end apart: 49, of which 20 were waited for; matrix products, arithmetic and copies ran while one was open for 12% of the time, Pallas kernels for 28%

profile of v1, /device:TPU:0, one launch (start us, length us, event | category | flops | bytes accessed | tf_op | source)
XLA Modules:
  0.0 283.7 jit_solution(5575987254994223248)
XLA Ops:
  0.7 3.0 %collective-permute-start = (bf16[128,4096]{1,0:T(8,128)(2,1)}, bf16[128,4096]{1,0:T(8,128)(2,1)S(1)}, u32[]{:S(2)}, u32[]{:S(2)}) collective-permute-start(bf16[128,4096]{1,0:T(8,128)(2,1)} %bitcast.50), channel_id=1, source_target_pairs={{0,1},{1,0},{2,3},{3,2},{4,5},{5,4},{6,7},{7,6},{8,9},{9,8},{10,11... | collective-permute-start | bytes 3145736 | tf_op jit(solution)/shard_map/ppermute | solution.py:20
  9.7 2.6 collective-permute-start.5
  17.1 10.0 %collective-permute-done.refs_1_ = bf16[128,4096]{1,0:T(8,128)(2,1)S(1)} collective-permute-done((bf16[128,4096]{1,0:T(8,128)(2,1)}, bf16[128,4096]{1,0:T(8,128)(2,1)S(1)}, u32[]{:S(2)}, u32[]{:S(2)}) %collective-permute-start) | collective-permute-done | bytes 1048608 | tf_op jit(solution)/shard_map/ppermute | solution.py:20
  35.3 6.9 %collective-permute-done.2.refs_3_ = bf16[64,4096]{1,0:T(8,128)(2,1)} collective-permute-done((bf16[64,4096]{1,0:T(8,128)(2,1)}, bf16[64,4096]{1,0:T(8,128)(2,1)}, u32[]{:S(2)}, u32[]{:S(2)}) %collective-permute-start.2) | collective-permute-done | bytes 524320 | tf_op jit(solution)/shard_map/ppermute | solution.py:20
  46.3 10.2 %shard_map.119 = (bf16[512,512]{1,0:T(8,128)(2,1)}, bf16[512,512]{1,0:T(8,128)(2,1)}, bf16[256,1024]{1,0:T(8,128)(2,1)}, bf16[256,1024]{1,0:T(8,128)(2,1)}, bf16...) custom-call(s32[1]{0:T(128)} %bitcast.core_ref, bf16[128,4096]{1,0:T(8,128)(2,1)S(1)} %bitcast.52, ...), custom_call_target="tpu_custom_call" | custom-call | flops 16777216 | bytes 1024 | tf_op jit(solution)/shard_map/pallas_call | solution.py:146
  63.6 6.4 %shard_map.120 = (bf16[512,4096]{1,0:T(8,128)(2,1)}, bf16[512,2048]{1,0:T(8,128)(2,1)}, bf16[512,512]{1,0:T(8,128)(2,1)}) custom-call(s32[1]{0:T(128)} %bitcast.core_ref, bf16[128,4096]{1,0:T(8,128)(2,1)S(1)} %bitcast.53, bf16[128,4096]{1,0:T(8,128)(2,1)S(1)} %collective-permute-done.refs_1_, bf16[128,4096]{1,0:T(8,128)(2,1)S(1)} %collective-permute-done.1.refs_2_, ...), custom_call_target="tpu_custom_call" | custom-call | flops 8388608 | bytes 1024 | tf_op jit(solution)/shard_map/pallas_call | solution.py:146
  76.5 10.1 %collective-permute-done.13 = bf16[256,512]{1,0:T(8,128)(2,1)S(1)} collective-permute-done((bf16[256,512]{1,0:T(8,128)(2,1)S(1)}, bf16[256,512]{1,0:T(8,128)(2,1)S(1)}, u32[]{:S(2)}, u32[]{:S(2)}) %collective-permute-start.13) | collective-permute-done | bytes 262176 | tf_op jit(solution)/shard_map/ppermute | solution.py:20
  88.1 3.2 %collective-permute-start.18 = (bf16[256,1024]{1,0:T(8,128)(2,1)}, bf16[256,1024]{1,0:T(8,128)(2,1)S(1)}, u32[]{:S(2)}, u32[]{:S(2)}) collective-permute-start(bf16[256,1024]{1,0:T(8,128)(2,1)} %get-tuple-element.261), channel_id=1, source_target_pairs={{0,4},{4,8},{8,12},{12,16},{16,20},{20,24},{24,28},{1,5},{5,9},{9,... | collective-permute-start | bytes 1572872 | tf_op jit(solution)/shard_map/ppermute | solution.py:775
  91.8 7.6 %shard_map.121 = (bf16[512,4096]{1,0:T(8,128)(2,1)}, bf16[512,2048]{1,0:T(8,128)(2,1)}, bf16[512,512]{1,0:T(8,128)(2,1)}) custom-call(s32[1]{0:T(128)} %bitcast.core_ref, bf16[128,4096]{1,0:T(8,128)(2,1)} %bitcast.54, bf16[64,4096]{1,0:T(8,128)(2,1)} %collective-permute-done.7.refs_1_, bf16[64,4096]{1,0:T(8,128)(2,1)} %collective-permute-done.11.refs_2_, ...), custom_call_target="tpu_custom_call" | custom-call | flops 8388608 | bytes 1024 | tf_op jit(solution)/shard_map/pallas_call | solution.py:146
  99.5 2.7 collective-permute-done.16
  105.7 7.4 %shard_map.122 = (bf16[512,512]{1,0:T(8,128)(2,1)}, bf16[512,512]{1,0:T(8,128)(2,1)}, f32[512,512]{1,0:T(8,128)}, f32[512,512]{1,0:T(8,128)}, bf16[256,1024]{1,0...) custom-call(s32[4,5]{1,0:T(4,128)S(1)} %concatenate.24.flags_ref, ...), custom_call_target="tpu_custom_call" | custom-call | flops 5505024 | bytes 1024 | tf_op jit(solution)/shard_map/pallas_call | solution.py:146
  121.5 4.7 %collective-permute-start.23 = (bf16[256,512]{1,0:T(8,128)(2,1)S(1)}, bf16[256,512]{1,0:T(8,128)(2,1)S(1)}, u32[]{:S(2)}, u32[]{:S(2)}) collective-permute-start(bf16[256,512]{1,0:T(8,128)(2,1)S(1)} %get-tuple-element.290), channel_id=1, source_target_pairs={{0,8},{4,12},{8,0},{12,4},{16,24},{20,28},{24,16},{28,20},{1,9},{5... | collective-permute-start | bytes 786440 | tf_op jit(solution)/shard_map/ppermute | solution.py:20
  126.2 12.2 %collective-permute-done.23 = bf16[256,512]{1,0:T(8,128)(2,1)S(1)} collective-permute-done((bf16[256,512]{1,0:T(8,128)(2,1)S(1)}, bf16[256,512]{1,0:T(8,128)(2,1)S(1)}, u32[]{:S(2)}, u32[]{:S(2)}) %collective-permute-start.23) | collective-permute-done | bytes 262176 | tf_op jit(solution)/shard_map/ppermute | solution.py:20
  138.5 4.0 %collective-permute-start.28 = (bf16[256,512]{1,0:T(8,128)(2,1)S(1)}, bf16[256,512]{1,0:T(8,128)(2,1)S(1)}, u32[]{:S(2)}, u32[]{:S(2)}) collective-permute-start(bf16[256,512]{1,0:T(8,128)(2,1)S(1)} %add.150), channel_id=1, source_target_pairs={{0,16},{4,20},{8,24},{12,28},{16,0},{20,4},{24,8},{28,12},{1,17},{... | collective-permute-start | bytes 786440 | tf_op jit(solution)/shard_map/ppermute | solution.py:20
  142.5 4.4 %shard_map.123 = (bf16[512,1024]{1,0:T(8,128)(2,1)}, bf16[512,1024]{1,0:T(8,128)(2,1)}) custom-call(s32[1]{0:T(128)} %bitcast.core_ref, bf16[512,512]{1,0:T(8,128)(2,1)} %get-tuple-element.286.dq_ref.q_ref, f32[512,512]{1,0:T(8,128)} %get-tuple-element.287.dk_ref, f32[512,512]{1,0:T(8,128)} %get-tuple-element.288.dv_ref, ...), custom_call_target="tpu_custom_call" | custom-call | flops 524288 | bytes 1024 | tf_op jit(solution)/shard_map/pallas_call | solution.py:146
  146.9 3.0 %collective-permute-done.28 = bf16[256,512]{1,0:T(8,128)(2,1)S(1)} collective-permute-done((bf16[256,512]{1,0:T(8,128)(2,1)S(1)}, bf16[256,512]{1,0:T(8,128)(2,1)S(1)}, u32[]{:S(2)}, u32[]{:S(2)}) %collective-permute-start.28) | collective-permute-done | bytes 262176 | tf_op jit(solution)/shard_map/ppermute | solution.py:20
  150.6 2.7 collective-permute-start.29
  156.7 9.9 %shard_map.124.terms_ref = bf16[4,512,1024]{2,1,0:T(8,128)(2,1)} custom-call(s32[1]{0:T(128)} %bitcast.core_ref, bf16[512,4096]{1,0:T(8,128)(2,1)} %get-tuple-element.300.c_ref, bf16[512,2048]{1,0:T(8,128)(2,1)} %copy-done.23, bf16[512,4096]{1,0:T(8,128)(2,1)} %get-tuple-element.302.x_ref, bf16[512,2048]{1,0:T(8,128)(2,1)} %copy-done.24, ...), custom_call_target="tpu_custom_call" | custom-call | flops 16777216 | bytes 1024 | tf_op jit(solution)/shard_map/pallas_call | solution.py:146
  166.6 9.3 %collective-permute-done.29.refs_8_ = bf16[512,1024]{1,0:T(8,128)(2,1)S(1)} collective-permute-done((bf16[512,1024]{1,0:T(8,128)(2,1)}, bf16[512,1024]{1,0:T(8,128)(2,1)S(1)}, u32[]{:S(2)}, u32[]{:S(2)}) %collective-permute-start.29) | collective-permute-done | bytes 1048608 | tf_op jit(solution)/shard_map/ppermute | solution.py:551
  175.9 4.1 %collective-permute-done.30.refs_9_ = bf16[512,1024]{1,0:T(8,128)(2,1)S(1)} collective-permute-done((bf16[512,1024]{1,0:T(8,128)(2,1)}, bf16[512,1024]{1,0:T(8,128)(2,1)S(1)}, u32[]{:S(2)}, u32[]{:S(2)}) %collective-permute-start.30) | collective-permute-done | bytes 1048608 | tf_op jit(solution)/shard_map/ppermute | solution.py:551
  182.2 3.6 %fusion.3 = (bf16[512,1024]{1,0:T(8,128)(2,1)S(1)}, bf16[512,1024]{1,0:T(8,128)(2,1)}) fusion(bf16[512,1024]{1,0:T(8,128)(2,1)S(1)} %collective-permute-done.30.refs_9_, bf16[4,512,1024]{2,1,0:T(8,128)(2,1)} %shard_map.124.terms_ref, s32[]{:T(128)S(6)} %select_n.349, pred[]{:T(512)S(6)} %eq.58, pred[]{:T(512)S(6)} %eq.57, ...), kind=kLoop, calls=%fused_computation.14 | loop fusion | flops 6291456 | bytes 6291468 | tf_op jit(solution)/shard_map/jit(_where)/select_n | solution.py:525
  195.3 4.6 %shard_map.125 = (bf16[512,512]{1,0:T(8,128)(2,1)}, bf16[512,512]{1,0:T(8,128)(2,1)}) custom-call(s32[1]{0:T(128)} %bitcast.core_ref, f32[512,512]{1,0:T(8,128)} %get-tuple-element.287.dk_ref, f32[512,512]{1,0:T(8,128)} %get-tuple-element.288.dv_ref, bf16[256,1024]{1,0:T(8,128)(2,1)} %copy-done.6, bf16[256,1024]{1,0:T(8,128)(2,1)} %copy-done.7, ...), custom_call_target="tpu_custom_call" | custom-call | flops 524288 | bytes 1024 | tf_op jit(solution)/shard_map/pallas_call | solution.py:146
  199.9 13.2 %shard_map.126 = (bf16[128,4096]{1,0:T(8,128)(2,1)}, bf16[128,4096]{1,0:T(8,128)(2,1)}, bf16[128,4096]{1,0:T(8,128)(2,1)}, bf16[64,4096]{1,0:T(8,128)(2,1)}, bf16[64,4096]{1,0:T(8,128)(2,1)}) custom-call(s32[1]{0:T(128)} %bitcast.core_ref, bf16[512,512]{1,0:T(8,128)(2,1)} %get-tuple-element.286.dq_ref.q_ref, bf16[512,512]{1,0:T(8,128)(2,1)} %get-tuple-element.313.k_ref, ...), custom_call_target="tpu_custom_call" | custom-call | flops 25165824 | bytes 1024 | tf_op jit(solution)/shard_map/pallas_call | solution.py:146
  217.7 4.5 %collective-permute-start.38 = (bf16[512,1024]{1,0:T(8,128)(2,1)}, bf16[512,1024]{1,0:T(8,128)(2,1)S(1)}, u32[]{:S(2)}, u32[]{:S(2)}) collective-permute-start(bf16[512,1024]{1,0:T(8,128)(2,1)} %get-tuple-element.329), channel_id=1, source_target_pairs={{0,8},{4,12},{8,16},{12,20},{16,24},{20,28},{1,9},{5,13},{9,17},{1... | collective-permute-start | bytes 3145736 | tf_op jit(solution)/shard_map/ppermute | solution.py:551
  226.0 3.3 %collective-permute-done.41 = bf16[64,4096]{1,0:T(8,128)(2,1)S(1)} collective-permute-done((bf16[64,4096]{1,0:T(8,128)(2,1)}, bf16[64,4096]{1,0:T(8,128)(2,1)S(1)}, u32[]{:S(2)}, u32[]{:S(2)}) %collective-permute-start.41) | collective-permute-done | bytes 524320 | tf_op jit(solution)/shard_map/ppermute | solution.py:20
  231.5 12.9 %collective-permute-done.38.refs_12_ = bf16[512,1024]{1,0:T(8,128)(2,1)S(1)} collective-permute-done((bf16[512,1024]{1,0:T(8,128)(2,1)}, bf16[512,1024]{1,0:T(8,128)(2,1)S(1)}, u32[]{:S(2)}, u32[]{:S(2)}) %collective-permute-start.38) | collective-permute-done | bytes 1048608 | tf_op jit(solution)/shard_map/ppermute | solution.py:551
  244.4 3.9 %collective-permute-done.39.refs_13_ = bf16[512,1024]{1,0:T(8,128)(2,1)S(1)} collective-permute-done((bf16[512,1024]{1,0:T(8,128)(2,1)S(1)}, bf16[512,1024]{1,0:T(8,128)(2,1)S(1)}, u32[]{:S(2)}, u32[]{:S(2)}) %collective-permute-start.39) | collective-permute-done | bytes 1048608 | tf_op jit(solution)/shard_map/ppermute | solution.py:551
  251.9 3.7 %collective-permute-start.44 = (bf16[512,1024]{1,0:T(8,128)(2,1)S(1)}, bf16[512,1024]{1,0:T(8,128)(2,1)S(1)}, u32[]{:S(2)}, u32[]{:S(2)}) collective-permute-start(bf16[512,1024]{1,0:T(8,128)(2,1)S(1)} %get-tuple-element.369), channel_id=1, source_target_pairs={{0,8},{4,12},{8,16},{12,20},{16,24},{20,28},{1,9},{5,13},{9,17},{1... | collective-permute-start | bytes 3145736 | tf_op jit(solution)/shard_map/ppermute | solution.py:551
  256.9 14.9 %shard_map.127 = (f32[512,1536]{1,0:T(8,128)}, bf16[512,512]{1,0:T(8,128)(2,1)}, bf16[512,512]{1,0:T(8,128)(2,1)}, bf16[512,512]{1,0:T(8,128)(2,1)}) custom-call(s32[9]{0:T(128)S(1)} %stack.58.slots_ref, bf16[4,1024,128]{2,1,0:T(8,128)(2,1)} %copy-done.16, bf16[4,1024,128]{2,1,0:T(8,128)(2,1)} %copy-done.17, bf16[4,1024,128]{2,1,0:T(8,128)(2,1)} %copy-done.19, ...), custom_call_target="tpu_custom_call" | custom-call | flops 29360128 | bytes 1024 | tf_op jit(solution)/shard_map/pallas_call | solution.py:146
  273.6 2.7 fusion.12
  276.9 3.1 %collective-permute-done.45.left_ref = bf16[512,1024]{1,0:T(8,128)(2,1)S(1)} collective-permute-done((bf16[512,1024]{1,0:T(8,128)(2,1)S(1)}, bf16[512,1024]{1,0:T(8,128)(2,1)S(1)}, u32[]{:S(2)}, u32[]{:S(2)}) %collective-permute-start.45) | collective-permute-done | bytes 1048608 | tf_op jit(solution)/shard_map/ppermute | solution.py:551
  280.0 3.7 %shard_map.128 = (f32[512,512]{1,0:T(8,128)}, f32[512,512]{1,0:T(8,128)}, f32[512,512]{1,0:T(8,128)}, f32[512,512]{1,0:T(8,128)}) custom-call(s32[1]{0:T(128)} %bitcast.33.chip_ref, bf16[4,512,1024]{2,1,0:T(8,128)(2,1)} %shard_map.124.terms_ref, bf16[512,1024]{1,0:T(8,128)(2,1)S(1)} %collective-permute-done.44.right_ref, ...), custom_call_target="tpu_custom_call" | custom-call | bytes 1024 | tf_op jit(solution)/shard_map/pallas_call | solution.py:146
  (201 shorter events, 83.9 us)
Async XLA Ops:
  0.7 26.4 %collective-permute-start = (bf16[128,4096]{1,0:T(8,128)(2,1)}, bf16[128,4096]{1,0:T(8,128)(2,1)S(1)}, u32[]{:S(2)}, u32[]{:S(2)}) collective-permute-start(bf16[128,4096]{1,0:T(8,128)(2,1)} %bitcast.50), channel_id=1, source_target_pairs={{0,1},{1,0},{2,3},{3,2},{4,5},{5,4},{6,7},{7,6},{8,9},{9,8},{10,11... | collective-permute-start | bytes 3145736 | tf_op jit(solution)/shard_map/ppermute | solution.py:20
  3.7 24.8 %collective-permute-start.1 = (bf16[128,4096]{1,0:T(8,128)(2,1)}, bf16[128,4096]{1,0:T(8,128)(2,1)S(1)}, u32[]{:S(2)}, u32[]{:S(2)}) collective-permute-start(bf16[128,4096]{1,0:T(8,128)(2,1)} %bitcast.51), channel_id=1, source_target_pairs={{0,2},{1,3},{2,0},{3,1},{4,6},{5,7},{6,4},{7,5},{8,10},{9,11},{10,... | collective-permute-start | bytes 3145736 | tf_op jit(solution)/shard_map/ppermute | solution.py:20
  7.3 28.0 %collective-permute-start.4 = (bf16[1024,128]{1,0:T(8,128)(2,1)}, bf16[1024,128]{1,0:T(8,128)(2,1)}, u32[]{:S(2)}, u32[]{:S(2)}) collective-permute-start(bf16[1024,128]{1,0:T(8,128)(2,1)} %bitcast.10), channel_id=1, source_target_pairs={{0,8},{4,12},{8,16},{12,20},{16,24},{20,28},{24,0},{28,4},{1,9},{5... | collective-permute-start | bytes 786440 | tf_op jit(solution)/shard_map/ppermute | solution.py:633
  9.7 25.6 %collective-permute-start.5 = (bf16[1024,128]{1,0:T(8,128)(2,1)}, bf16[1024,128]{1,0:T(8,128)(2,1)}, u32[]{:S(2)}, u32[]{:S(2)}) collective-permute-start(bf16[1024,128]{1,0:T(8,128)(2,1)} %bitcast.12), channel_id=1, source_target_pairs={{0,16},{4,20},{8,24},{12,28},{16,0},{20,4},{24,8},{28,12},{1,17},{... | collective-permute-start | bytes 786440 | tf_op jit(solution)/shard_map/ppermute | solution.py:633
  13.1 22.2 %collective-permute-start.6 = (bf16[1024,128]{1,0:T(8,128)(2,1)}, bf16[1024,128]{1,0:T(8,128)(2,1)}, u32[]{:S(2)}, u32[]{:S(2)}) collective-permute-start(bf16[1024,128]{1,0:T(8,128)(2,1)} %bitcast.14), channel_id=1, source_target_pairs={{0,24},{4,28},{8,0},{12,4},{16,8},{20,12},{24,16},{28,20},{1,25},{... | collective-permute-start | bytes 786440 | tf_op jit(solution)/shard_map/ppermute | solution.py:633
  43.5 13.1 %collective-permute-start.7 = (bf16[64,4096]{1,0:T(8,128)(2,1)}, bf16[64,4096]{1,0:T(8,128)(2,1)}, u32[]{:S(2)}, u32[]{:S(2)}) collective-permute-start(bf16[64,4096]{1,0:T(8,128)(2,1)} %get-tuple-element.210), channel_id=1, source_target_pairs={{0,1},{1,0},{2,3},{3,2},{4,5},{5,4},{6,7},{7,6},{8,9},{9,8},{10,11... | collective-permute-start | bytes 1572872 | tf_op jit(solution)/shard_map/ppermute | solution.py:20
  56.6 15.1 %collective-permute-start.11 = (bf16[64,4096]{1,0:T(8,128)(2,1)}, bf16[64,4096]{1,0:T(8,128)(2,1)}, u32[]{:S(2)}, u32[]{:S(2)}) collective-permute-start(bf16[64,4096]{1,0:T(8,128)(2,1)} %get-tuple-element.218), channel_id=1, source_target_pairs={{0,1},{1,0},{2,3},{3,2},{4,5},{5,4},{6,7},{7,6},{8,9},{9,8},{10,11... | collective-permute-start | bytes 1572872 | tf_op jit(solution)/shard_map/ppermute | solution.py:20
  57.3 14.4 %collective-permute-start.12 = (bf16[64,4096]{1,0:T(8,128)(2,1)}, bf16[64,4096]{1,0:T(8,128)(2,1)}, u32[]{:S(2)}, u32[]{:S(2)}) collective-permute-start(bf16[64,4096]{1,0:T(8,128)(2,1)} %get-tuple-element.218), channel_id=1, source_target_pairs={{0,2},{1,3},{2,0},{3,1},{4,6},{5,7},{6,4},{7,5},{8,10},{9,11},{10,... | collective-permute-start | bytes 1572872 | tf_op jit(solution)/shard_map/ppermute | solution.py:20
  62.7 24.0 %collective-permute-start.14 = (bf16[64,4096]{1,0:T(8,128)(2,1)}, bf16[64,4096]{1,0:T(8,128)(2,1)S(1)}, u32[]{:S(2)}, u32[]{:S(2)}) collective-permute-start(bf16[64,4096]{1,0:T(8,128)(2,1)} %collective-permute-done.8.refs_3_), channel_id=1, source_target_pairs={{0,1},{1,0},{2,3},{3,2},{4,5},{5,4},{6,7},{7,6},{8,9},{9,8},{10,11... | collective-permute-start | bytes 1572872 | tf_op jit(solution)/shard_map/ppermute | solution.py:20
  71.7 15.0 %collective-permute-start.15 = (bf16[64,4096]{1,0:T(8,128)(2,1)}, bf16[64,4096]{1,0:T(8,128)(2,1)S(1)}, u32[]{:S(2)}, u32[]{:S(2)}) collective-permute-start(bf16[64,4096]{1,0:T(8,128)(2,1)} %collective-permute-done.11.refs_2_), channel_id=1, source_target_pairs={{0,2},{1,3},{2,0},{3,1},{4,6},{5,7},{6,4},{7,5},{8,10},{9,11},{10,... | collective-permute-start | bytes 1572872 | tf_op jit(solution)/shard_map/ppermute | solution.py:20
  72.8 13.9 %collective-permute-start.13 = (bf16[256,512]{1,0:T(8,128)(2,1)S(1)}, bf16[256,512]{1,0:T(8,128)(2,1)S(1)}, u32[]{:S(2)}, u32[]{:S(2)}) collective-permute-start(bf16[256,512]{1,0:T(8,128)(2,1)S(1)} %dynamic-slice_add_fusion), channel_id=1, source_target_pairs={{0,16},{4,20},{8,24},{12,28},{16,0},{20,4},{24,8},{28,12},{1,17},{... | collective-permute-start | bytes 786440 | tf_op jit(solution)/shard_map/ppermute | solution.py:20
  86.7 15.7 %collective-permute-start.17 = (bf16[256,1024]{1,0:T(8,128)(2,1)}, bf16[256,1024]{1,0:T(8,128)(2,1)S(1)}, u32[]{:S(2)}, u32[]{:S(2)}) collective-permute-start(bf16[256,1024]{1,0:T(8,128)(2,1)} %get-tuple-element.260), channel_id=1, source_target_pairs={{4,0},{8,4},{12,8},{16,12},{20,16},{24,20},{28,24},{5,1},{9,5},{13... | collective-permute-start | bytes 1572872 | tf_op jit(solution)/shard_map/ppermute | solution.py:774
  88.1 14.4 %collective-permute-start.18 = (bf16[256,1024]{1,0:T(8,128)(2,1)}, bf16[256,1024]{1,0:T(8,128)(2,1)S(1)}, u32[]{:S(2)}, u32[]{:S(2)}) collective-permute-start(bf16[256,1024]{1,0:T(8,128)(2,1)} %get-tuple-element.261), channel_id=1, source_target_pairs={{0,4},{4,8},{8,12},{12,16},{16,20},{20,24},{24,28},{1,5},{5,9},{9,... | collective-permute-start | bytes 1572872 | tf_op jit(solution)/shard_map/ppermute | solution.py:775
  114.8 32.1 %collective-permute-start.26 = (bf16[4,1024,128]{2,1,0:T(8,128)(2,1)S(1)}, bf16[4,1024,128]{2,1,0:T(8,128)(2,1)S(1)}, u32[]{:S(2)}, u32[]{:S(2)}) collective-permute-start(bf16[4,1024,128]{2,1,0:T(8,128)(2,1)S(1)} %pad_maximum_fusion.refs_0_), channel_id=1, source_target_pairs={{0,1},{1,0},{2,3},{3,2},{4,5},{5,4},{6,7},{7,6},{8,9},{9,8},{10,11... | collective-permute-start | bytes 3145736 | tf_op jit(solution)/shard_map/ppermute | solution.py:20
  116.2 30.7 %collective-permute-start.27 = (bf16[4,1024,128]{2,1,0:T(8,128)(2,1)S(1)}, bf16[4,1024,128]{2,1,0:T(8,128)(2,1)S(1)}, u32[]{:S(2)}, u32[]{:S(2)}) collective-permute-start(bf16[4,1024,128]{2,1,0:T(8,128)(2,1)S(1)} %pad_maximum_fusion.refs_0_), channel_id=1, source_target_pairs={{0,2},{1,3},{2,0},{3,1},{4,6},{5,7},{6,4},{7,5},{8,10},{9,11},{10,... | collective-permute-start | bytes 3145736 | tf_op jit(solution)/shard_map/ppermute | solution.py:20
  118.4 24.1 %collective-permute-start.24 = (bf16[256,1024]{1,0:T(8,128)(2,1)S(1)}, bf16[256,1024]{1,0:T(8,128)(2,1)S(1)}, u32[]{:S(2)}, u32[]{:S(2)}) collective-permute-start(bf16[256,1024]{1,0:T(8,128)(2,1)S(1)} %copy-done.36), channel_id=1, source_target_pairs={{0,4},{4,8},{8,12},{12,16},{16,20},{20,24},{24,28},{1,5},{5,9},{9,... | collective-permute-start | bytes 1572872 | tf_op jit(solution)/shard_map/ppermute | solution.py:817
  120.2 22.3 %collective-permute-start.25 = (bf16[256,1024]{1,0:T(8,128)(2,1)S(1)}, bf16[256,1024]{1,0:T(8,128)(2,1)S(1)}, u32[]{:S(2)}, u32[]{:S(2)}) collective-permute-start(bf16[256,1024]{1,0:T(8,128)(2,1)S(1)} %copy-done.35), channel_id=1, source_target_pairs={{4,0},{8,4},{12,8},{16,12},{20,16},{24,20},{28,24},{5,1},{9,5},{13... | collective-permute-start | bytes 1572872 | tf_op jit(solution)/shard_map/ppermute | solution.py:816
  121.5 17.0 %collective-permute-start.23 = (bf16[256,512]{1,0:T(8,128)(2,1)S(1)}, bf16[256,512]{1,0:T(8,128)(2,1)S(1)}, u32[]{:S(2)}, u32[]{:S(2)}) collective-permute-start(bf16[256,512]{1,0:T(8,128)(2,1)S(1)} %get-tuple-element.290), channel_id=1, source_target_pairs={{0,8},{4,12},{8,0},{12,4},{16,24},{20,28},{24,16},{28,20},{1,9},{5... | collective-permute-start | bytes 786440 | tf_op jit(solution)/shard_map/ppermute | solution.py:20
  150.6 25.3 %collective-permute-start.29 = (bf16[512,1024]{1,0:T(8,128)(2,1)}, bf16[512,1024]{1,0:T(8,128)(2,1)S(1)}, u32[]{:S(2)}, u32[]{:S(2)}) collective-permute-start(bf16[512,1024]{1,0:T(8,128)(2,1)} %get-tuple-element.299.refs_7_), channel_id=1, source_target_pairs={{0,8},{4,12},{8,16},{12,20},{16,24},{20,28},{1,9},{5,13},{9,17},{1... | collective-permute-start | bytes 3145736 | tf_op jit(solution)/shard_map/ppermute | solution.py:551
  153.3 26.7 %collective-permute-start.30 = (bf16[512,1024]{1,0:T(8,128)(2,1)}, bf16[512,1024]{1,0:T(8,128)(2,1)S(1)}, u32[]{:S(2)}, u32[]{:S(2)}) collective-permute-start(bf16[512,1024]{1,0:T(8,128)(2,1)} %get-tuple-element.299.refs_7_), channel_id=1, source_target_pairs={{24,16},{28,20},{16,8},{20,12},{8,0},{12,4},{25,17},{29,21},{17,9}... | collective-permute-start | bytes 3145736 | tf_op jit(solution)/shard_map/ppermute | solution.py:551
  185.8 27.4 %collective-permute-start.32 = (bf16[512,1024]{1,0:T(8,128)(2,1)}, bf16[512,1024]{1,0:T(8,128)(2,1)S(1)}, u32[]{:S(2)}, u32[]{:S(2)}) collective-permute-start(bf16[512,1024]{1,0:T(8,128)(2,1)} %get-tuple-element.390), channel_id=1, source_target_pairs={{0,8},{4,12},{8,16},{12,20},{16,24},{20,28},{1,9},{5,13},{9,17},{1... | collective-permute-start | bytes 3145736 | tf_op jit(solution)/shard_map/ppermute | solution.py:551
  188.3 25.6 %collective-permute-start.33 = (bf16[512,1024]{1,0:T(8,128)(2,1)S(1)}, bf16[512,1024]{1,0:T(8,128)(2,1)S(1)}, u32[]{:S(2)}, u32[]{:S(2)}) collective-permute-start(bf16[512,1024]{1,0:T(8,128)(2,1)S(1)} %get-tuple-element.389), channel_id=1, source_target_pairs={{24,16},{28,20},{16,8},{20,12},{8,0},{12,4},{25,17},{29,21},{17,9}... | collective-permute-start | bytes 3145736 | tf_op jit(solution)/shard_map/ppermute | solution.py:551
  191.4 21.7 %collective-permute-start.36 = (bf16[2,1024,128]{2,1,0:T(8,128)(2,1)}, bf16[2,1024,128]{2,1,0:T(8,128)(2,1)}, u32[]{:S(2)}, u32[]{:S(2)}) collective-permute-start(bf16[2,1024,128]{2,1,0:T(8,128)(2,1)} %slice.35), channel_id=1, source_target_pairs={{0,1},{1,0},{2,3},{3,2},{4,5},{5,4},{6,7},{7,6},{8,9},{9,8},{10,11... | collective-permute-start | bytes 1572872 | tf_op jit(solution)/shard_map/ppermute | solution.py:20
  193.1 20.0 %collective-permute-start.37 = (bf16[2,1024,128]{2,1,0:T(8,128)(2,1)}, bf16[2,1024,128]{2,1,0:T(8,128)(2,1)}, u32[]{:S(2)}, u32[]{:S(2)}) collective-permute-start(bf16[2,1024,128]{2,1,0:T(8,128)(2,1)} %slice.34), channel_id=1, source_target_pairs={{0,2},{1,3},{2,0},{3,1},{4,6},{5,7},{6,4},{7,5},{8,10},{9,11},{10,... | collective-permute-start | bytes 1572872 | tf_op jit(solution)/shard_map/ppermute | solution.py:20
  216.0 13.3 %collective-permute-start.41 = (bf16[64,4096]{1,0:T(8,128)(2,1)}, bf16[64,4096]{1,0:T(8,128)(2,1)S(1)}, u32[]{:S(2)}, u32[]{:S(2)}) collective-permute-start(bf16[64,4096]{1,0:T(8,128)(2,1)} %get-tuple-element.342), channel_id=1, source_target_pairs={{0,1},{1,0},{2,3},{3,2},{4,5},{5,4},{6,7},{7,6},{8,9},{9,8},{10,11... | collective-permute-start | bytes 1572872 | tf_op jit(solution)/shard_map/ppermute | solution.py:20
  216.8 13.6 %collective-permute-start.40 = (bf16[64,4096]{1,0:T(8,128)(2,1)}, bf16[64,4096]{1,0:T(8,128)(2,1)S(1)}, u32[]{:S(2)}, u32[]{:S(2)}) collective-permute-start(bf16[64,4096]{1,0:T(8,128)(2,1)} %get-tuple-element.340), channel_id=1, source_target_pairs={{0,2},{1,3},{2,0},{3,1},{4,6},{5,7},{6,4},{7,5},{8,10},{9,11},{10,... | collective-permute-start | bytes 1572872 | tf_op jit(solution)/shard_map/ppermute | solution.py:20
  217.7 26.7 %collective-permute-start.38 = (bf16[512,1024]{1,0:T(8,128)(2,1)}, bf16[512,1024]{1,0:T(8,128)(2,1)S(1)}, u32[]{:S(2)}, u32[]{:S(2)}) collective-permute-start(bf16[512,1024]{1,0:T(8,128)(2,1)} %get-tuple-element.329), channel_id=1, source_target_pairs={{0,8},{4,12},{8,16},{12,20},{16,24},{20,28},{1,9},{5,13},{9,17},{1... | collective-permute-start | bytes 3145736 | tf_op jit(solution)/shard_map/ppermute | solution.py:551
  222.2 26.1 %collective-permute-start.39 = (bf16[512,1024]{1,0:T(8,128)(2,1)S(1)}, bf16[512,1024]{1,0:T(8,128)(2,1)S(1)}, u32[]{:S(2)}, u32[]{:S(2)}) collective-permute-start(bf16[512,1024]{1,0:T(8,128)(2,1)S(1)} %get-tuple-element.330), channel_id=1, source_target_pairs={{24,16},{28,20},{16,8},{20,12},{8,0},{12,4},{25,17},{29,21},{17,9}... | collective-permute-start | bytes 3145736 | tf_op jit(solution)/shard_map/ppermute | solution.py:551
  249.4 23.5 %collective-permute-start.42 = (bf16[128,4096]{1,0:T(8,128)(2,1)}, bf16[128,4096]{1,0:T(8,128)(2,1)S(1)}, u32[]{:S(2)}, u32[]{:S(2)}) collective-permute-start(bf16[128,4096]{1,0:T(8,128)(2,1)} %add_convert_fusion.4), channel_id=1, source_target_pairs={{0,1},{1,0},{2,3},{3,2},{4,5},{5,4},{6,7},{7,6},{8,9},{9,8},{10,11... | collective-permute-start | bytes 3145736 | tf_op jit(solution)/shard_map/ppermute | solution.py:20
  250.3 23.3 %collective-permute-start.43 = (bf16[128,4096]{1,0:T(8,128)(2,1)}, bf16[128,4096]{1,0:T(8,128)(2,1)}, u32[]{:S(2)}, u32[]{:S(2)}) collective-permute-start(bf16[128,4096]{1,0:T(8,128)(2,1)} %add_convert_fusion.3), channel_id=1, source_target_pairs={{0,2},{1,3},{2,0},{3,1},{4,6},{5,7},{6,4},{7,5},{8,10},{9,11},{10,... | collective-permute-start | bytes 3145736 | tf_op jit(solution)/shard_map/ppermute | solution.py:20
  251.9 24.9 %collective-permute-start.44 = (bf16[512,1024]{1,0:T(8,128)(2,1)S(1)}, bf16[512,1024]{1,0:T(8,128)(2,1)S(1)}, u32[]{:S(2)}, u32[]{:S(2)}) collective-permute-start(bf16[512,1024]{1,0:T(8,128)(2,1)S(1)} %get-tuple-element.369), channel_id=1, source_target_pairs={{0,8},{4,12},{8,16},{12,20},{16,24},{20,28},{1,9},{5,13},{9,17},{1... | collective-permute-start | bytes 3145736 | tf_op jit(solution)/shard_map/ppermute | solution.py:551
  255.7 24.3 %collective-permute-start.45 = (bf16[512,1024]{1,0:T(8,128)(2,1)S(1)}, bf16[512,1024]{1,0:T(8,128)(2,1)S(1)}, u32[]{:S(2)}, u32[]{:S(2)}) collective-permute-start(bf16[512,1024]{1,0:T(8,128)(2,1)S(1)} %get-tuple-element.370), channel_id=1, source_target_pairs={{24,16},{28,20},{16,8},{20,12},{8,0},{12,4},{25,17},{29,21},{17,9}... | collective-permute-start | bytes 3145736 | tf_op jit(solution)/shard_map/ppermute | solution.py:551
  (56 other events, 475.6 us)

commit v2 on v1

--- a/solution.py
+++ b/solution.py
@@ -384,14 +384,12 @@
 
 
 def finish_kernel(
-    core_ref, dq_ref, dk_ref, dv_ref, ctx_ref, before_ref, after_ref, keys_ref, values_ref
+    core_ref, dk_ref, dv_ref, ctx_ref, before_ref, after_ref, keys_ref, values_ref
 ):
     rows, width = dk_ref.shape
-    keys_ref[:, :width] = dq_ref[...]
     values_ref[:, :width] = ctx_ref[...]
-    cols = slice(width, 2 * width)
-    for own_ref, shift, out_ref in ((dk_ref, 0, keys_ref), (dv_ref, width, values_ref)):
-        side = slice(shift, shift + width)
+    for own_ref, shift, out_ref, to in ((dk_ref, 0, keys_ref, 0), (dv_ref, width, values_ref, width)):
+        side, cols = slice(shift, shift + width), slice(to, to + width)
         out_ref[:BLOCK, cols] = (own_ref[:BLOCK] + before_ref[:, side].astype(F32)).astype(BF16)
         if rows > 2 * BLOCK:
             out_ref[BLOCK : rows - BLOCK, cols] = own_ref[BLOCK : rows - BLOCK].astype(BF16)
@@ -509,7 +507,7 @@
     def pieces(self):
         chosen, pieces, table = self.schedule[len(self.received)], [], []
         count = self.chips
-        plain = len(self.firsts) > 1 and len(self.received) == 1 and self.size == self.shape == (self.rows, self.wide)
+        plain = len(self.received) == 1 and self.size == self.shape == (self.rows, self.wide)
         for way, sign in enumerate((1, -1)):
             place = self.place(sign)
             sums = [int(chosen.get(c, ("", 0))[0] == "sum") for c in range(count)]
@@ -532,8 +530,12 @@
             functools.partial(pieces_kernel, len(arrived[0])),
             (4,),
             jnp.stack(table),
-            [(self.partial, pl.BlockSpec((1, part, wide), lambda i, t, at=at: (t[at], i, 0))) for at in (0, 3)]
-            + [(a, pl.BlockSpec((part, a.shape[1]), lambda i, *_: (i, 0))) for way in arrived for a in way],
+            [(self.partial, pl.BlockSpec((1, part, wide), lambda i, t, at=at: (t[at], i * t[at + 1], 0))) for at in (0, 3)]
+            + [
+                (a, pl.BlockSpec((part, a.shape[1]), lambda i, t, at=at: (i * (1 - t[at + 1] * t[at + 2]), 0)))
+                for at, way in zip((0, 3), arrived)
+                for a in way
+            ],
             [((rows, wide), BF16, pl.BlockSpec((part, wide), lambda i, *_: (i, 0)))] * 2,
             0,
             space=jax.ShapeDtypeStruct,
@@ -589,34 +591,38 @@
         )
 
 
-def final_kernel(
-    chip_ref, terms_ref, right_ref, left_ref, mine_ref, *refs
-):
-    others, (q_ref, k_ref, v_ref, o_ref) = refs[:3], refs[3:]
-    width, size = q_ref.shape[1], o_ref.shape[1]
-    rows, wide = terms_ref.shape[1:]
-    summed = terms_ref[0].astype(F32)
-    summed += right_ref[:rows, :wide].astype(F32)
-    summed += left_ref[:rows, :wide].astype(F32)
-    o_ref[...] = summed[:, :size]
+def final_kernel(chip_ref, *refs):
+    sums, (mine_ref, *others), (q_ref, k_ref, v_ref, o_ref) = refs[:6], refs[6:10], refs[10:]
+    width = q_ref.shape[1]
+    for refs, out_ref in ((sums[0::2], o_ref), (sums[1::2], None)):
+        total = refs[0][0].astype(F32) + refs[1][...].astype(F32) + refs[2][...].astype(F32)
+        if out_ref is not None:
+            out_ref[...] = total
     q_ref[...] = mine_ref[:, :width] + others[0][...].astype(F32)
     k_ref[...] = mine_ref[:, width : 2 * width] + others[1][...].astype(F32)
-    v_ref[...] = mine_ref[:, 2 * width :] + others[2][...].astype(F32) + summed[:, size:].T
+    v_ref[...] = mine_ref[:, 2 * width :] + others[2][...].astype(F32) + total.T
 
 
 def final_sums(line, mine, others, width):
-    _, rows, wide = line.partial.shape
-    size = mine.shape[0]
+    rows, size, part = line.partial.shape[1], mine.shape[0], 128
+    skip = size // part
+    ins = [
+        (line.partial, pl.BlockSpec((1, part, size), lambda i, c: (c[0], i, 0))),
+        (line.partial, pl.BlockSpec((1, rows, part), lambda i, c: (c[0], 0, skip + i))),
+    ]
+    for came in line.received[-1]:
+        ins.append((came, pl.BlockSpec((part, size), lambda i, *_: (i, 0))))
+        ins.append((came, pl.BlockSpec((rows, part), lambda i, *_: (0, skip + i))))
+    by_part = lambda wide: pl.BlockSpec((part, wide), lambda i, *_: (i, 0))
     return call(
         final_kernel,
-        (1,),
+        (skip,),
         line.chip.reshape(1),
-        [(line.partial, pl.BlockSpec((1, rows, wide), lambda i, c: (c[0], 0, 0)))]
-        + [(a, fixed(a.shape)) for a in (*line.received[-1], mine, *others)],
-        [((size, width), F32, fixed((size, width)))] * 3 + [((rows, size), F32, fixed((rows, size)))],
+        ins + [(a, by_part(a.shape[1])) for a in (mine, *others)],
+        [((size, width), F32, by_part(width))] * 3 + [((rows, size), F32, by_part(size))],
         0,
         limit=32,
-        free=range(1, 7),
+        free=range(2, 10),
     )
 
 
@@ -815,6 +821,7 @@
     given = swap(given, "seq", CORES)
     from_after = lax.ppermute(dbefore, "seq", shift_pairs(n_seq, -1))
     from_before = lax.ppermute(dafter, "seq", shift_pairs(n_seq, 1))
+    line.begin(grad_q)
     dglob, context = phase((kept + given, context))
     dglob, came = sum_second(dglob, chips)
     to_gather, to_scatter = call(
@@ -823,14 +830,14 @@
         core.reshape(1),
         [
             (a, by_doc(a.shape[0] // docs, a.shape[1]))
-            for a in (grad_q, dkey, dvalue, context, from_before, from_after)
+            for a in (dkey, dvalue, context, from_before, from_after)
         ],
-        [((docs * rows, 2 * width), BF16, by_doc(rows, 2 * width))] * 2,
+        [((docs * rows, k * width), BF16, by_doc(rows, k * width)) for k in (1, 2)],
         4 * docs * rows * globs * width,
-        free=(4, 5),
-    )
-    to_gather, to_scatter, columns, near_columns, came = phase(
-        (to_gather, to_scatter, columns, near_columns, came)
+        free=(3, 4),
+    )
+    to_gather, to_scatter, columns, near_columns, came, line.firsts = phase(
+        (to_gather, to_scatter, columns, near_columns, came, line.firsts)
     )
     dglob = dglob + came
 

time: 285 us -> 283 us (level)
  starting transfers between devices: 70.8 us -> 77.1 us
  waiting for transfers between devices: 89.3 us -> 83.8 us
  other arithmetic: 24.2 us -> 19.4 us
  Pallas kernels: 82.3 us -> 86.4 us
    ppermute x8 -> x10, waiting for transfers between devices: 33.9 us -> 23 us  [move(): got.append(lax.ppermute(piece, 'seq', pairs))]
    ppermute x34, waiting for transfers between devices: 55.4 us -> 60.8 us  [swap(): lax.ppermute(value, axis, [(i, i ^ mask) for i in range(lax.axis_size(axi...]
    ppermute x34, starting transfers between devices: 38.9 us -> 43.6 us  [swap(): lax.ppermute(value, axis, [(i, i ^ mask) for i in range(lax.axis_size(axi...]
    pallas_call x10 -> x11, Pallas kernels: 82.3 us -> 86.4 us  [call(): pl.pallas_call(kernel, grid_spec=pltpu.PrefetchScalarGridSpec(num_scalar_...]
    select_n x3 -> x2, other arithmetic: 6.75 us -> 3.11 us  [pieces(): jnp.where(lookup(place, sums) == 1, jnp.where(place == 0, own, added), be...]
    ppermute x8 -> x10, starting transfers between devices: 18.8 us -> 20.4 us  [move(): got.append(lax.ppermute(piece, 'seq', pairs))]
  transfers between devices with their start and end apart: 49 -> 51, of which waited for: 20 -> 21; matrix products, arithmetic and copies ran while one was open for 12% -> 10% of each run, Pallas kernels for 28% -> 29%
where the time goes in v2:
time: 283 us; the launch traced here: 282 us
  Pallas kernels  86.4 us (31%)
  waiting for transfers between devices  83.8 us (30%)
  starting transfers between devices  77.1 us (27%)
  other arithmetic  19.4 us (7%)
  local copies, waits for them, and re-layouts  13.8 us (5%)
    pallas_call x11, Pallas kernels, call(): pl.pallas_call(kernel, grid_spec=pltpu.PrefetchScalarGridSpec(num_scalar_...  86.4 us
    ppermute x34, waiting for transfers between devices, swap(): lax.ppermute(value, axis, [(i, i ^ mask) for i in range(lax.axis_size(axi...  60.8 us
    ppermute x34, starting transfers between devices, swap(): lax.ppermute(value, axis, [(i, i ^ mask) for i in range(lax.axis_size(axi...  43.6 us
    ppermute x10, waiting for transfers between devices, move(): got.append(lax.ppermute(piece, 'seq', pairs))  23 us
    ppermute x10, starting transfers between devices, move(): got.append(lax.ppermute(piece, 'seq', pairs))  20.4 us
  transfers between devices with their start and end apart: 51, of which 21 were waited for; matrix products, arithmetic and copies ran while one was open for 10% of the time, Pallas kernels for 29%

profile of v2, /device:TPU:0, one launch (start us, length us, event | category | flops | bytes accessed | tf_op | source)
XLA Modules:
  0.0 282.0 jit_solution(2808814338300611227)
XLA Ops:
  0.7 3.0 %collective-permute-start = (bf16[128,4096]{1,0:T(8,128)(2,1)}, bf16[128,4096]{1,0:T(8,128)(2,1)S(1)}, u32[]{:S(2)}, u32[]{:S(2)}) collective-permute-start(bf16[128,4096]{1,0:T(8,128)(2,1)} %bitcast.52), channel_id=1, source_target_pairs={{0,1},{1,0},{2,3},{3,2},{4,5},{5,4},{6,7},{7,6},{8,9},{9,8},{10,11... | collective-permute-start | bytes 3145736 | tf_op jit(solution)/shard_map/ppermute | solution.py:20
  9.7 2.6 collective-permute-start.5
  17.1 10.0 %collective-permute-done.refs_1_ = bf16[128,4096]{1,0:T(8,128)(2,1)S(1)} collective-permute-done((bf16[128,4096]{1,0:T(8,128)(2,1)}, bf16[128,4096]{1,0:T(8,128)(2,1)S(1)}, u32[]{:S(2)}, u32[]{:S(2)}) %collective-permute-start) | collective-permute-done | bytes 1048608 | tf_op jit(solution)/shard_map/ppermute | solution.py:20
  35.3 6.9 %collective-permute-done.2.refs_3_ = bf16[64,4096]{1,0:T(8,128)(2,1)} collective-permute-done((bf16[64,4096]{1,0:T(8,128)(2,1)}, bf16[64,4096]{1,0:T(8,128)(2,1)}, u32[]{:S(2)}, u32[]{:S(2)}) %collective-permute-start.2) | collective-permute-done | bytes 524320 | tf_op jit(solution)/shard_map/ppermute | solution.py:20
  46.3 10.2 %shard_map.119 = (bf16[512,512]{1,0:T(8,128)(2,1)}, bf16[512,512]{1,0:T(8,128)(2,1)}, bf16[256,1024]{1,0:T(8,128)(2,1)}, bf16[256,1024]{1,0:T(8,128)(2,1)}, bf16...) custom-call(s32[1]{0:T(128)} %bitcast.core_ref, bf16[128,4096]{1,0:T(8,128)(2,1)S(1)} %bitcast.54, ...), custom_call_target="tpu_custom_call" | custom-call | flops 16777216 | bytes 1024 | tf_op jit(solution)/shard_map/pallas_call | solution.py:146
  64.2 6.4 %shard_map.120 = (bf16[512,4096]{1,0:T(8,128)(2,1)}, bf16[512,2048]{1,0:T(8,128)(2,1)}, bf16[512,512]{1,0:T(8,128)(2,1)}) custom-call(s32[1]{0:T(128)} %bitcast.core_ref, bf16[128,4096]{1,0:T(8,128)(2,1)S(1)} %bitcast.55, bf16[128,4096]{1,0:T(8,128)(2,1)S(1)} %collective-permute-done.refs_1_, bf16[128,4096]{1,0:T(8,128)(2,1)S(1)} %collective-permute-done.1.refs_2_, ...), custom_call_target="tpu_custom_call" | custom-call | flops 8388608 | bytes 1024 | tf_op jit(solution)/shard_map/pallas_call | solution.py:146
  72.8 2.6 collective-permute-start.13
  76.6 10.1 %collective-permute-done.13 = bf16[256,512]{1,0:T(8,128)(2,1)S(1)} collective-permute-done((bf16[256,512]{1,0:T(8,128)(2,1)S(1)}, bf16[256,512]{1,0:T(8,128)(2,1)S(1)}, u32[]{:S(2)}, u32[]{:S(2)}) %collective-permute-start.13) | collective-permute-done | bytes 262176 | tf_op jit(solution)/shard_map/ppermute | solution.py:20
  88.1 3.2 %collective-permute-start.18 = (bf16[256,1024]{1,0:T(8,128)(2,1)}, bf16[256,1024]{1,0:T(8,128)(2,1)S(1)}, u32[]{:S(2)}, u32[]{:S(2)}) collective-permute-start(bf16[256,1024]{1,0:T(8,128)(2,1)} %get-tuple-element.267), channel_id=1, source_target_pairs={{0,4},{4,8},{8,12},{12,16},{16,20},{20,24},{24,28},{1,5},{5,9},{9,... | collective-permute-start | bytes 1572872 | tf_op jit(solution)/shard_map/ppermute | solution.py:781
  92.1 7.7 %shard_map.121 = (bf16[512,4096]{1,0:T(8,128)(2,1)}, bf16[512,2048]{1,0:T(8,128)(2,1)}, bf16[512,512]{1,0:T(8,128)(2,1)}) custom-call(s32[1]{0:T(128)} %bitcast.core_ref, bf16[128,4096]{1,0:T(8,128)(2,1)} %bitcast.56, bf16[64,4096]{1,0:T(8,128)(2,1)} %collective-permute-done.7.refs_1_, bf16[64,4096]{1,0:T(8,128)(2,1)} %collective-permute-done.11.refs_2_, ...), custom_call_target="tpu_custom_call" | custom-call | flops 8388608 | bytes 1024 | tf_op jit(solution)/shard_map/pallas_call | solution.py:146
  99.8 2.6 collective-permute-done.16
  105.9 7.4 %shard_map.122 = (bf16[512,512]{1,0:T(8,128)(2,1)}, bf16[512,512]{1,0:T(8,128)(2,1)}, f32[512,512]{1,0:T(8,128)}, f32[512,512]{1,0:T(8,128)}, bf16[256,1024]{1,0...) custom-call(s32[4,5]{1,0:T(4,128)S(1)} %concatenate.26.flags_ref, ...), custom_call_target="tpu_custom_call" | custom-call | flops 5505024 | bytes 1024 | tf_op jit(solution)/shard_map/pallas_call | solution.py:146
  119.1 2.4 collective-permute-start.23
  122.8 5.4 %collective-permute-done.23 = bf16[256,512]{1,0:T(8,128)(2,1)S(1)} collective-permute-done((bf16[256,512]{1,0:T(8,128)(2,1)S(1)}, bf16[256,512]{1,0:T(8,128)(2,1)S(1)}, u32[]{:S(2)}, u32[]{:S(2)}) %collective-permute-start.23) | collective-permute-done | bytes 262176 | tf_op jit(solution)/shard_map/ppermute | solution.py:20
  128.1 4.4 %collective-permute-start.29 = (bf16[512,512]{1,0:T(8,128)(2,1)S(1)}, bf16[512,512]{1,0:T(8,128)(2,1)S(1)}, u32[]{:S(2)}, u32[]{:S(2)}) collective-permute-start(bf16[512,512]{1,0:T(8,128)(2,1)S(1)} %copy-done.27), channel_id=1, source_target_pairs={{0,8},{4,12},{8,16},{12,20},{16,24},{20,28},{1,9},{5,13},{9,17},{1... | collective-permute-start | bytes 1572872 | tf_op jit(solution)/shard_map/ppermute | solution.py:553
  134.0 4.0 %collective-permute-start.28 = (bf16[256,512]{1,0:T(8,128)(2,1)S(1)}, bf16[256,512]{1,0:T(8,128)(2,1)S(1)}, u32[]{:S(2)}, u32[]{:S(2)}) collective-permute-start(bf16[256,512]{1,0:T(8,128)(2,1)S(1)} %add.139), channel_id=1, source_target_pairs={{0,16},{4,20},{8,24},{12,28},{16,0},{20,4},{24,8},{28,12},{1,17},{... | collective-permute-start | bytes 786440 | tf_op jit(solution)/shard_map/ppermute | solution.py:20
  138.0 3.8 %shard_map.123 = (bf16[512,512]{1,0:T(8,128)(2,1)}, bf16[512,1024]{1,0:T(8,128)(2,1)}) custom-call(s32[1]{0:T(128)} %bitcast.core_ref, f32[512,512]{1,0:T(8,128)} %get-tuple-element.287.dk_ref, f32[512,512]{1,0:T(8,128)} %get-tuple-element.288.dv_ref, bf16[512,512]{1,0:T(8,128)(2,1)} %get-tuple-element.297.ctx_ref, ...), custom_call_target="tpu_custom_call" | custom-call | flops 524288 | bytes 1024 | tf_op jit(solution)/shard_map/pallas_call | solution.py:146
  141.8 13.0 %collective-permute-done.28 = bf16[256,512]{1,0:T(8,128)(2,1)S(1)} collective-permute-done((bf16[256,512]{1,0:T(8,128)(2,1)S(1)}, bf16[256,512]{1,0:T(8,128)(2,1)S(1)}, u32[]{:S(2)}, u32[]{:S(2)}) %collective-permute-start.28) | collective-permute-done | bytes 262176 | tf_op jit(solution)/shard_map/ppermute | solution.py:20
  154.8 6.9 %collective-permute-start.33 = (bf16[512,1024]{1,0:T(8,128)(2,1)}, bf16[512,1024]{1,0:T(8,128)(2,1)S(1)}, u32[]{:S(2)}, u32[]{:S(2)}) collective-permute-start(bf16[512,1024]{1,0:T(8,128)(2,1)} %get-tuple-element.312.g_ref), channel_id=1, source_target_pairs={{0,4},{4,0},{8,12},{12,8},{16,20},{20,16},{24,28},{28,24},{1,5},{5... | collective-permute-start | bytes 3145736 | tf_op jit(solution)/shard_map/ppermute | solution.py:20
  165.4 9.9 %shard_map.124.right_ref.left_ref.refs_0_.refs_1_ = bf16[4,512,1024]{2,1,0:T(8,128)(2,1)} custom-call(s32[1]{0:T(128)} %bitcast.core_ref, bf16[512,4096]{1,0:T(8,128)(2,1)} %get-tuple-element.308.c_ref, bf16[512,2048]{1,0:T(8,128)(2,1)} %copy-done.25, bf16[512,4096]{1,0:T(8,128)(2,1)} %get-tuple-element.310.x_ref, bf16[512,2048]{1,0:T(8,128)(2,1)} %copy-done.26, ...), custom_call_target="tpu_custom_call" | custom-call | flops 16777216 | bytes 1024 | tf_op jit(solution)/shard_map/pallas_call | solution.py:146
  175.3 3.7 %collective-permute-done.32.refs_3_.refs_12_ = bf16[512,512]{1,0:T(8,128)(2,1)S(1)} collective-permute-done((bf16[512,512]{1,0:T(8,128)(2,1)}, bf16[512,512]{1,0:T(8,128)(2,1)S(1)}, u32[]{:S(2)}, u32[]{:S(2)}) %collective-permute-start.32) | collective-permute-done | bytes 524320 | tf_op jit(solution)/shard_map/ppermute | solution.py:553
  179.8 4.3 %shard_map.125 = (bf16[512,1024]{1,0:T(8,128)(2,1)}, bf16[512,1024]{1,0:T(8,128)(2,1)}) custom-call(s32[6]{0:T(128)S(1)} %stack.86.table_ref, bf16[4,512,1024]{2,1,0:T(8,128)(2,1)} %shard_map.124.right_ref.left_ref.refs_0_.refs_1_, bf16[4,512,1024]{2,1,0:T(8,128)(2,1)} %shard_map.124.right_ref.left_ref.refs_0_.refs_1_, ...), custom_call_target="tpu_custom_call" | custom-call | bytes 1024 | tf_op jit(solution)/shard_map/pallas_call | solution.py:146
  184.2 2.7 collective-permute-start.34
  193.4 4.5 %shard_map.126 = (bf16[512,512]{1,0:T(8,128)(2,1)}, bf16[512,512]{1,0:T(8,128)(2,1)}) custom-call(s32[1]{0:T(128)} %bitcast.core_ref, f32[512,512]{1,0:T(8,128)} %get-tuple-element.287.dk_ref, f32[512,512]{1,0:T(8,128)} %get-tuple-element.288.dv_ref, bf16[256,1024]{1,0:T(8,128)(2,1)} %copy-done.6, bf16[256,1024]{1,0:T(8,128)(2,1)} %copy-done.7, ...), custom_call_target="tpu_custom_call" | custom-call | flops 524288 | bytes 1024 | tf_op jit(solution)/shard_map/pallas_call | solution.py:146
  197.9 13.3 %shard_map.127 = (bf16[128,4096]{1,0:T(8,128)(2,1)}, bf16[128,4096]{1,0:T(8,128)(2,1)}, bf16[128,4096]{1,0:T(8,128)(2,1)}, bf16[64,4096]{1,0:T(8,128)(2,1)}, bf16[64,4096]{1,0:T(8,128)(2,1)}) custom-call(s32[1]{0:T(128)} %bitcast.core_ref, bf16[512,512]{1,0:T(8,128)(2,1)} %get-tuple-element.304.q_ref.refs_7_, bf16[512,512]{1,0:T(8,128)(2,1)} %get-tuple-element.325.k_ref, ...), custom_call_target="tpu_custom_call" | custom-call | flops 25165824 | bytes 1024 | tf_op jit(solution)/shard_map/pallas_call | solution.py:146
  216.9 3.0 %collective-permute-start.40 = (bf16[512,1024]{1,0:T(8,128)(2,1)}, bf16[512,1024]{1,0:T(8,128)(2,1)S(1)}, u32[]{:S(2)}, u32[]{:S(2)}) collective-permute-start(bf16[512,1024]{1,0:T(8,128)(2,1)} %get-tuple-element.341), channel_id=1, source_target_pairs={{0,8},{4,12},{8,16},{12,20},{16,24},{20,28},{1,9},{5,13},{9,17},{1... | collective-permute-start | bytes 3145736 | tf_op jit(solution)/shard_map/ppermute | solution.py:553
  223.6 3.7 %collective-permute-done.43 = bf16[64,4096]{1,0:T(8,128)(2,1)S(1)} collective-permute-done((bf16[64,4096]{1,0:T(8,128)(2,1)}, bf16[64,4096]{1,0:T(8,128)(2,1)S(1)}, u32[]{:S(2)}, u32[]{:S(2)}) %collective-permute-start.43) | collective-permute-done | bytes 524320 | tf_op jit(solution)/shard_map/ppermute | solution.py:20
  229.5 12.5 %collective-permute-done.40.refs_15_ = bf16[512,1024]{1,0:T(8,128)(2,1)S(1)} collective-permute-done((bf16[512,1024]{1,0:T(8,128)(2,1)}, bf16[512,1024]{1,0:T(8,128)(2,1)S(1)}, u32[]{:S(2)}, u32[]{:S(2)}) %collective-permute-start.40) | collective-permute-done | bytes 1048608 | tf_op jit(solution)/shard_map/ppermute | solution.py:553
  242.0 3.9 %collective-permute-done.41.refs_16_ = bf16[512,1024]{1,0:T(8,128)(2,1)S(1)} collective-permute-done((bf16[512,1024]{1,0:T(8,128)(2,1)S(1)}, bf16[512,1024]{1,0:T(8,128)(2,1)S(1)}, u32[]{:S(2)}, u32[]{:S(2)}) %collective-permute-start.41) | collective-permute-done | bytes 1048608 | tf_op jit(solution)/shard_map/ppermute | solution.py:553
  253.6 14.8 %shard_map.128 = (f32[512,1536]{1,0:T(8,128)}, bf16[512,512]{1,0:T(8,128)(2,1)}, bf16[512,512]{1,0:T(8,128)(2,1)}, bf16[512,512]{1,0:T(8,128)(2,1)}) custom-call(s32[9]{0:T(128)S(1)} %stack.94.slots_ref, bf16[4,1024,128]{2,1,0:T(8,128)(2,1)} %copy-done.18, bf16[4,1024,128]{2,1,0:T(8,128)(2,1)} %copy-done.19, bf16[4,1024,128]{2,1,0:T(8,128)(2,1)} %copy-done.21, ...), custom_call_target="tpu_custom_call" | custom-call | flops 29360128 | bytes 1024 | tf_op jit(solution)/shard_map/pallas_call | solution.py:146
  271.6 2.7 fusion.8
  277.7 4.1 %shard_map.129 = (f32[512,512]{1,0:T(8,128)}, f32[512,512]{1,0:T(8,128)}, f32[512,512]{1,0:T(8,128)}, f32[512,512]{1,0:T(8,128)}) custom-call(s32[1]{0:T(128)} %bitcast.37.chip_ref, bf16[4,512,1024]{2,1,0:T(8,128)(2,1)} %shard_map.124.right_ref.left_ref.refs_0_.refs_1_, bf16[4,512,1024]{2,1,0:T(8,128)(2,1)} %shard_map.124.right_ref.left_ref.refs_0_.refs_1_, ...), custom_call_target="tpu_custom_call" | custom-call | bytes 1024 | tf_op jit(solution)/shard_map/pallas_call | solution.py:146
  (210 shorter events, 85.1 us)
Async XLA Ops:
  0.7 26.4 %collective-permute-start = (bf16[128,4096]{1,0:T(8,128)(2,1)}, bf16[128,4096]{1,0:T(8,128)(2,1)S(1)}, u32[]{:S(2)}, u32[]{:S(2)}) collective-permute-start(bf16[128,4096]{1,0:T(8,128)(2,1)} %bitcast.52), channel_id=1, source_target_pairs={{0,1},{1,0},{2,3},{3,2},{4,5},{5,4},{6,7},{7,6},{8,9},{9,8},{10,11... | collective-permute-start | bytes 3145736 | tf_op jit(solution)/shard_map/ppermute | solution.py:20
  3.7 24.8 %collective-permute-start.1 = (bf16[128,4096]{1,0:T(8,128)(2,1)}, bf16[128,4096]{1,0:T(8,128)(2,1)S(1)}, u32[]{:S(2)}, u32[]{:S(2)}) collective-permute-start(bf16[128,4096]{1,0:T(8,128)(2,1)} %bitcast.53), channel_id=1, source_target_pairs={{0,2},{1,3},{2,0},{3,1},{4,6},{5,7},{6,4},{7,5},{8,10},{9,11},{10,... | collective-permute-start | bytes 3145736 | tf_op jit(solution)/shard_map/ppermute | solution.py:20
  7.3 28.0 %collective-permute-start.4 = (bf16[1024,128]{1,0:T(8,128)(2,1)}, bf16[1024,128]{1,0:T(8,128)(2,1)}, u32[]{:S(2)}, u32[]{:S(2)}) collective-permute-start(bf16[1024,128]{1,0:T(8,128)(2,1)} %bitcast.10), channel_id=1, source_target_pairs={{0,8},{4,12},{8,16},{12,20},{16,24},{20,28},{24,0},{28,4},{1,9},{5... | collective-permute-start | bytes 786440 | tf_op jit(solution)/shard_map/ppermute | solution.py:639
  9.7 25.6 %collective-permute-start.5 = (bf16[1024,128]{1,0:T(8,128)(2,1)}, bf16[1024,128]{1,0:T(8,128)(2,1)}, u32[]{:S(2)}, u32[]{:S(2)}) collective-permute-start(bf16[1024,128]{1,0:T(8,128)(2,1)} %bitcast.12), channel_id=1, source_target_pairs={{0,16},{4,20},{8,24},{12,28},{16,0},{20,4},{24,8},{28,12},{1,17},{... | collective-permute-start | bytes 786440 | tf_op jit(solution)/shard_map/ppermute | solution.py:639
  13.1 22.2 %collective-permute-start.6 = (bf16[1024,128]{1,0:T(8,128)(2,1)}, bf16[1024,128]{1,0:T(8,128)(2,1)}, u32[]{:S(2)}, u32[]{:S(2)}) collective-permute-start(bf16[1024,128]{1,0:T(8,128)(2,1)} %bitcast.14), channel_id=1, source_target_pairs={{0,24},{4,28},{8,0},{12,4},{16,8},{20,12},{24,16},{28,20},{1,25},{... | collective-permute-start | bytes 786440 | tf_op jit(solution)/shard_map/ppermute | solution.py:639
  30.5 12.9 %collective-permute-start.3 = (bf16[64,4096]{1,0:T(8,128)(2,1)}, bf16[64,4096]{1,0:T(8,128)(2,1)}, u32[]{:S(2)}, u32[]{:S(2)}) collective-permute-start(bf16[64,4096]{1,0:T(8,128)(2,1)} %slice.29), channel_id=1, source_target_pairs={{0,2},{1,3},{2,0},{3,1},{4,6},{5,7},{6,4},{7,5},{8,10},{9,11},{10,... | collective-permute-start | bytes 1572872 | tf_op jit(solution)/shard_map/ppermute | solution.py:20
  43.5 13.1 %collective-permute-start.7 = (bf16[64,4096]{1,0:T(8,128)(2,1)}, bf16[64,4096]{1,0:T(8,128)(2,1)}, u32[]{:S(2)}, u32[]{:S(2)}) collective-permute-start(bf16[64,4096]{1,0:T(8,128)(2,1)} %get-tuple-element.216), channel_id=1, source_target_pairs={{0,1},{1,0},{2,3},{3,2},{4,5},{5,4},{6,7},{7,6},{8,9},{9,8},{10,11... | collective-permute-start | bytes 1572872 | tf_op jit(solution)/shard_map/ppermute | solution.py:20
  56.6 15.1 %collective-permute-start.11 = (bf16[64,4096]{1,0:T(8,128)(2,1)}, bf16[64,4096]{1,0:T(8,128)(2,1)}, u32[]{:S(2)}, u32[]{:S(2)}) collective-permute-start(bf16[64,4096]{1,0:T(8,128)(2,1)} %get-tuple-element.224), channel_id=1, source_target_pairs={{0,1},{1,0},{2,3},{3,2},{4,5},{5,4},{6,7},{7,6},{8,9},{9,8},{10,11... | collective-permute-start | bytes 1572872 | tf_op jit(solution)/shard_map/ppermute | solution.py:20
  57.3 14.4 %collective-permute-start.12 = (bf16[64,4096]{1,0:T(8,128)(2,1)}, bf16[64,4096]{1,0:T(8,128)(2,1)}, u32[]{:S(2)}, u32[]{:S(2)}) collective-permute-start(bf16[64,4096]{1,0:T(8,128)(2,1)} %get-tuple-element.224), channel_id=1, source_target_pairs={{0,2},{1,3},{2,0},{3,1},{4,6},{5,7},{6,4},{7,5},{8,10},{9,11},{10,... | collective-permute-start | bytes 1572872 | tf_op jit(solution)/shard_map/ppermute | solution.py:20
  63.3 23.4 %collective-permute-start.14 = (bf16[64,4096]{1,0:T(8,128)(2,1)}, bf16[64,4096]{1,0:T(8,128)(2,1)S(1)}, u32[]{:S(2)}, u32[]{:S(2)}) collective-permute-start(bf16[64,4096]{1,0:T(8,128)(2,1)} %collective-permute-done.8.refs_3_), channel_id=1, source_target_pairs={{0,1},{1,0},{2,3},{3,2},{4,5},{5,4},{6,7},{7,6},{8,9},{9,8},{10,11... | collective-permute-start | bytes 1572872 | tf_op jit(solution)/shard_map/ppermute | solution.py:20
  71.7 15.0 %collective-permute-start.15 = (bf16[64,4096]{1,0:T(8,128)(2,1)}, bf16[64,4096]{1,0:T(8,128)(2,1)S(1)}, u32[]{:S(2)}, u32[]{:S(2)}) collective-permute-start(bf16[64,4096]{1,0:T(8,128)(2,1)} %collective-permute-done.11.refs_2_), channel_id=1, source_target_pairs={{0,2},{1,3},{2,0},{3,1},{4,6},{5,7},{6,4},{7,5},{8,10},{9,11},{10,... | collective-permute-start | bytes 1572872 | tf_op jit(solution)/shard_map/ppermute | solution.py:20
  72.8 13.9 %collective-permute-start.13 = (bf16[256,512]{1,0:T(8,128)(2,1)S(1)}, bf16[256,512]{1,0:T(8,128)(2,1)S(1)}, u32[]{:S(2)}, u32[]{:S(2)}) collective-permute-start(bf16[256,512]{1,0:T(8,128)(2,1)S(1)} %dynamic-slice_add_fusion), channel_id=1, source_target_pairs={{0,16},{4,20},{8,24},{12,28},{16,0},{20,4},{24,8},{28,12},{1,17},{... | collective-permute-start | bytes 786440 | tf_op jit(solution)/shard_map/ppermute | solution.py:20
  86.8 15.8 %collective-permute-start.17 = (bf16[256,1024]{1,0:T(8,128)(2,1)}, bf16[256,1024]{1,0:T(8,128)(2,1)S(1)}, u32[]{:S(2)}, u32[]{:S(2)}) collective-permute-start(bf16[256,1024]{1,0:T(8,128)(2,1)} %get-tuple-element.266), channel_id=1, source_target_pairs={{4,0},{8,4},{12,8},{16,12},{20,16},{24,20},{28,24},{5,1},{9,5},{13... | collective-permute-start | bytes 1572872 | tf_op jit(solution)/shard_map/ppermute | solution.py:780
  88.1 14.5 %collective-permute-start.18 = (bf16[256,1024]{1,0:T(8,128)(2,1)}, bf16[256,1024]{1,0:T(8,128)(2,1)S(1)}, u32[]{:S(2)}, u32[]{:S(2)}) collective-permute-start(bf16[256,1024]{1,0:T(8,128)(2,1)} %get-tuple-element.267), channel_id=1, source_target_pairs={{0,4},{4,8},{8,12},{12,16},{16,20},{20,24},{24,28},{1,5},{5,9},{9,... | collective-permute-start | bytes 1572872 | tf_op jit(solution)/shard_map/ppermute | solution.py:781
  113.8 28.0 %collective-permute-start.26 = (bf16[4,1024,128]{2,1,0:T(8,128)(2,1)S(1)}, bf16[4,1024,128]{2,1,0:T(8,128)(2,1)S(1)}, u32[]{:S(2)}, u32[]{:S(2)}) collective-permute-start(bf16[4,1024,128]{2,1,0:T(8,128)(2,1)S(1)} %pad_maximum_fusion.refs_0_), channel_id=1, source_target_pairs={{0,1},{1,0},{2,3},{3,2},{4,5},{5,4},{6,7},{7,6},{8,9},{9,8},{10,11... | collective-permute-start | bytes 3145736 | tf_op jit(solution)/shard_map/ppermute | solution.py:20
  115.1 26.7 %collective-permute-start.27 = (bf16[4,1024,128]{2,1,0:T(8,128)(2,1)S(1)}, bf16[4,1024,128]{2,1,0:T(8,128)(2,1)S(1)}, u32[]{:S(2)}, u32[]{:S(2)}) collective-permute-start(bf16[4,1024,128]{2,1,0:T(8,128)(2,1)S(1)} %pad_maximum_fusion.refs_0_), channel_id=1, source_target_pairs={{0,2},{1,3},{2,0},{3,1},{4,6},{5,7},{6,4},{7,5},{8,10},{9,11},{10,... | collective-permute-start | bytes 3145736 | tf_op jit(solution)/shard_map/ppermute | solution.py:20
  117.3 15.2 %collective-permute-start.24 = (bf16[256,1024]{1,0:T(8,128)(2,1)S(1)}, bf16[256,1024]{1,0:T(8,128)(2,1)S(1)}, u32[]{:S(2)}, u32[]{:S(2)}) collective-permute-start(bf16[256,1024]{1,0:T(8,128)(2,1)S(1)} %copy-done.38), channel_id=1, source_target_pairs={{0,4},{4,8},{8,12},{12,16},{16,20},{20,24},{24,28},{1,5},{5,9},{9,... | collective-permute-start | bytes 1572872 | tf_op jit(solution)/shard_map/ppermute | solution.py:823
  128.1 26.7 %collective-permute-start.29 = (bf16[512,512]{1,0:T(8,128)(2,1)S(1)}, bf16[512,512]{1,0:T(8,128)(2,1)S(1)}, u32[]{:S(2)}, u32[]{:S(2)}) collective-permute-start(bf16[512,512]{1,0:T(8,128)(2,1)S(1)} %copy-done.27), channel_id=1, source_target_pairs={{0,8},{4,12},{8,16},{12,20},{16,24},{20,28},{1,9},{5,13},{9,17},{1... | collective-permute-start | bytes 1572872 | tf_op jit(solution)/shard_map/ppermute | solution.py:553
  132.6 22.3 %collective-permute-start.30 = (bf16[512,512]{1,0:T(8,128)(2,1)S(1)}, bf16[512,512]{1,0:T(8,128)(2,1)S(1)}, u32[]{:S(2)}, u32[]{:S(2)}) collective-permute-start(bf16[512,512]{1,0:T(8,128)(2,1)S(1)} %copy-done.27), channel_id=1, source_target_pairs={{24,16},{28,20},{16,8},{20,12},{8,0},{12,4},{25,17},{29,21},{17,9}... | collective-permute-start | bytes 1572872 | tf_op jit(solution)/shard_map/ppermute | solution.py:553
  134.0 20.9 %collective-permute-start.28 = (bf16[256,512]{1,0:T(8,128)(2,1)S(1)}, bf16[256,512]{1,0:T(8,128)(2,1)S(1)}, u32[]{:S(2)}, u32[]{:S(2)}) collective-permute-start(bf16[256,512]{1,0:T(8,128)(2,1)S(1)} %add.139), channel_id=1, source_target_pairs={{0,16},{4,20},{8,24},{12,28},{16,0},{20,4},{24,8},{28,12},{1,17},{... | collective-permute-start | bytes 786440 | tf_op jit(solution)/shard_map/ppermute | solution.py:20
  161.8 13.6 %collective-permute-start.31 = (bf16[512,512]{1,0:T(8,128)(2,1)}, bf16[512,512]{1,0:T(8,128)(2,1)S(1)}, u32[]{:S(2)}, u32[]{:S(2)}) collective-permute-start(bf16[512,512]{1,0:T(8,128)(2,1)} %get-tuple-element.307.refs_8_), channel_id=1, source_target_pairs={{0,8},{4,12},{8,16},{12,20},{16,24},{20,28},{1,9},{5,13},{9,17},{1... | collective-permute-start | bytes 1572872 | tf_op jit(solution)/shard_map/ppermute | solution.py:553
  163.1 16.0 %collective-permute-start.32 = (bf16[512,512]{1,0:T(8,128)(2,1)}, bf16[512,512]{1,0:T(8,128)(2,1)S(1)}, u32[]{:S(2)}, u32[]{:S(2)}) collective-permute-start(bf16[512,512]{1,0:T(8,128)(2,1)} %get-tuple-element.307.refs_8_), channel_id=1, source_target_pairs={{24,16},{28,20},{16,8},{20,12},{8,0},{12,4},{25,17},{29,21},{17,9}... | collective-permute-start | bytes 1572872 | tf_op jit(solution)/shard_map/ppermute | solution.py:553
  184.2 27.0 %collective-permute-start.34 = (bf16[512,1024]{1,0:T(8,128)(2,1)}, bf16[512,1024]{1,0:T(8,128)(2,1)S(1)}, u32[]{:S(2)}, u32[]{:S(2)}) collective-permute-start(bf16[512,1024]{1,0:T(8,128)(2,1)} %get-tuple-element.319), channel_id=1, source_target_pairs={{0,8},{4,12},{8,16},{12,20},{16,24},{20,28},{1,9},{5,13},{9,17},{1... | collective-permute-start | bytes 3145736 | tf_op jit(solution)/shard_map/ppermute | solution.py:553
  186.8 25.8 %collective-permute-start.35 = (bf16[512,1024]{1,0:T(8,128)(2,1)}, bf16[512,1024]{1,0:T(8,128)(2,1)S(1)}, u32[]{:S(2)}, u32[]{:S(2)}) collective-permute-start(bf16[512,1024]{1,0:T(8,128)(2,1)} %get-tuple-element.320), channel_id=1, source_target_pairs={{24,16},{28,20},{16,8},{20,12},{8,0},{12,4},{25,17},{29,21},{17,9}... | collective-permute-start | bytes 3145736 | tf_op jit(solution)/shard_map/ppermute | solution.py:553
  189.2 22.0 %collective-permute-start.38 = (bf16[2,1024,128]{2,1,0:T(8,128)(2,1)S(1)}, bf16[2,1024,128]{2,1,0:T(8,128)(2,1)}, u32[]{:S(2)}, u32[]{:S(2)}) collective-permute-start(bf16[2,1024,128]{2,1,0:T(8,128)(2,1)S(1)} %slice.35), channel_id=1, source_target_pairs={{0,1},{1,0},{2,3},{3,2},{4,5},{5,4},{6,7},{7,6},{8,9},{9,8},{10,11... | collective-permute-start | bytes 1572872 | tf_op jit(solution)/shard_map/ppermute | solution.py:20
  191.4 19.8 %collective-permute-start.39 = (bf16[2,1024,128]{2,1,0:T(8,128)(2,1)}, bf16[2,1024,128]{2,1,0:T(8,128)(2,1)}, u32[]{:S(2)}, u32[]{:S(2)}) collective-permute-start(bf16[2,1024,128]{2,1,0:T(8,128)(2,1)} %slice.34), channel_id=1, source_target_pairs={{0,2},{1,3},{2,0},{3,1},{4,6},{5,7},{6,4},{7,5},{8,10},{9,11},{10,... | collective-permute-start | bytes 1572872 | tf_op jit(solution)/shard_map/ppermute | solution.py:20
  216.9 25.2 %collective-permute-start.40 = (bf16[512,1024]{1,0:T(8,128)(2,1)}, bf16[512,1024]{1,0:T(8,128)(2,1)S(1)}, u32[]{:S(2)}, u32[]{:S(2)}) collective-permute-start(bf16[512,1024]{1,0:T(8,128)(2,1)} %get-tuple-element.341), channel_id=1, source_target_pairs={{0,8},{4,12},{8,16},{12,20},{16,24},{20,28},{1,9},{5,13},{9,17},{1... | collective-permute-start | bytes 3145736 | tf_op jit(solution)/shard_map/ppermute | solution.py:553
  219.8 26.1 %collective-permute-start.41 = (bf16[512,1024]{1,0:T(8,128)(2,1)S(1)}, bf16[512,1024]{1,0:T(8,128)(2,1)S(1)}, u32[]{:S(2)}, u32[]{:S(2)}) collective-permute-start(bf16[512,1024]{1,0:T(8,128)(2,1)S(1)} %get-tuple-element.342), channel_id=1, source_target_pairs={{24,16},{28,20},{16,8},{20,12},{8,0},{12,4},{25,17},{29,21},{17,9}... | collective-permute-start | bytes 3145736 | tf_op jit(solution)/shard_map/ppermute | solution.py:553
  247.0 23.5 %collective-permute-start.44 = (bf16[128,4096]{1,0:T(8,128)(2,1)}, bf16[128,4096]{1,0:T(8,128)(2,1)S(1)}, u32[]{:S(2)}, u32[]{:S(2)}) collective-permute-start(bf16[128,4096]{1,0:T(8,128)(2,1)} %add_convert_fusion.4), channel_id=1, source_target_pairs={{0,1},{1,0},{2,3},{3,2},{4,5},{5,4},{6,7},{7,6},{8,9},{9,8},{10,11... | collective-permute-start | bytes 3145736 | tf_op jit(solution)/shard_map/ppermute | solution.py:20
  248.3 23.3 %collective-permute-start.45 = (bf16[128,4096]{1,0:T(8,128)(2,1)}, bf16[128,4096]{1,0:T(8,128)(2,1)}, u32[]{:S(2)}, u32[]{:S(2)}) collective-permute-start(bf16[128,4096]{1,0:T(8,128)(2,1)} %add_convert_fusion.3), channel_id=1, source_target_pairs={{0,2},{1,3},{2,0},{3,1},{4,6},{5,7},{6,4},{7,5},{8,10},{9,11},{10,... | collective-permute-start | bytes 3145736 | tf_op jit(solution)/shard_map/ppermute | solution.py:20
  250.0 24.9 %collective-permute-start.46 = (bf16[512,1024]{1,0:T(8,128)(2,1)S(1)}, bf16[512,1024]{1,0:T(8,128)(2,1)S(1)}, u32[]{:S(2)}, u32[]{:S(2)}) collective-permute-start(bf16[512,1024]{1,0:T(8,128)(2,1)S(1)} %get-tuple-element.381), channel_id=1, source_target_pairs={{0,8},{4,12},{8,16},{12,20},{16,24},{20,28},{1,9},{5,13},{9,17},{1... | collective-permute-start | bytes 3145736 | tf_op jit(solution)/shard_map/ppermute | solution.py:553
  252.3 24.2 %collective-permute-start.47 = (bf16[512,1024]{1,0:T(8,128)(2,1)S(1)}, bf16[512,1024]{1,0:T(8,128)(2,1)S(1)}, u32[]{:S(2)}, u32[]{:S(2)}) collective-permute-start(bf16[512,1024]{1,0:T(8,128)(2,1)S(1)} %get-tuple-element.382), channel_id=1, source_target_pairs={{24,16},{28,20},{16,8},{20,12},{8,0},{12,4},{25,17},{29,21},{17,9}... | collective-permute-start | bytes 3145736 | tf_op jit(solution)/shard_map/ppermute | solution.py:553
  (60 other events, 625.4 us)
